TPU v7x, 32 devices: a whole 2x2x4 slice. The times are simulated.
32 devices in a mesh: rep: 2 (over x), section: 2 (over core), tp: 8 (over z, y).
Axes of the slice: x: 2, y: 2, z: 4, core: 2. Of those that a mesh axis runs over, the one named last changes fastest.
Arguments:
- queries: bfloat16 [2, 16, 64, 128], P('section', 'rep', 'tp'), parts along dimension 1, may hold values from -200 to 200
- new_kv: bfloat16 [2, 16, 2, 4, 128], P('section', 'rep'), parts along dimension 1, may hold values from -6 to 6
- kv_cache: bfloat16 [2, 16, 2, 4, 1024, 128], P('section', 'rep', None, None, 'tp'), parts along dimension 1, may hold values from -6 to 6
- lengths: int32 [2, 16], P('section', 'rep'), parts along dimension 1, may hold values from 2 to 1023, as said below
- residual: bfloat16 [2, 16, 16384], P('section', 'rep', 'tp'), parts along dimension 1, may hold values from -3 to 3
- out_weight: bfloat16 [2, 8192, 16384], P('section', 'tp'), may hold values from -0.09375 to 0.09375
Outputs:
- handed: bfloat16 [2, 16, 16384], P('section', 'rep'), parts along dimension 1
There are 2 independent parts, one for each index of `rep`. A program takes and returns all parts, laid end to end along the dimension named above; an argument that names none is the same for every part. Nothing has to cross between parts.
Inputs may be any that keep to these rules, and one draw needn't show every extreme that they name: Row r attends to cached positions 0 to lengths - 1 and to its new token at position lengths; in each section some row has the largest value.
All inputs are finite; a program needn't handle non-finite values.
Results may differ from a plain program's by a relative error of at most 0.039.
Values may be sent and summed in bfloat16 or wider, within the bound.
No kernel may reach another device: no remote copies, remote signals or barrier semaphores. Data moves between devices by JAX's collectives and lax.ppermute only.
A program may use at most 192 MiB of HBM per device.

v0:
```python
import functools
import math

import jax
import jax.numpy as jnp
from jax import lax
from jax.experimental import pallas as pl
from jax.experimental.pallas import tpu as pltpu
from jax.sharding import PartitionSpec as P

QB = 128
LANES = 128
STAT_ROWS = 16
MIB = 1 << 20
F32 = jnp.float32
BF16 = jnp.bfloat16
VMEM_SPEC = pl.BlockSpec(memory_space=pltpu.VMEM)
ANY_SPEC = pl.BlockSpec(memory_space=pl.ANY)


def pieces(x):
    high = x.astype(BF16).astype(F32)
    rest = x - high
    middle = rest.astype(BF16).astype(F32)
    return high, middle, rest - middle


def weight_copies(units, weight_ref, held_ref, sems):
    rank = lax.axis_index("tp")
    columns = held_ref.shape[2]
    copies = []
    for i, (slot, half) in enumerate(units):
        start = pl.multiple_of(((rank ^ slot) * 2 + half) * columns, columns)
        copies.append(
            pltpu.make_async_copy(
                weight_ref.at[0, :, pl.ds(start, columns)], held_ref.at[i], sems.at[i]
            )
        )
    return copies


def stage_cache_kernel(
    per, units, lengths_ref, new_ref, kv_ref, queries_ref, weight_ref,
    stored_ref, limit_ref, near_ref, held_ref, lengths, new, kv, sems, held_sems,
):
    rank = lax.axis_index("tp")
    rows, _, kv_heads, span, dim = kv.shape
    copies = [
        pltpu.make_async_copy(lengths_ref, lengths, sems.at[0]),
        pltpu.make_async_copy(new_ref.at[0], new, sems.at[1]),
        pltpu.make_async_copy(kv_ref.at[0], kv, sems.at[2]),
        pltpu.make_async_copy(queries_ref, near_ref, sems.at[3]),
    ]
    held = weight_copies(units, weight_ref, held_ref, held_sems)
    for copy in copies + held:
        copy.start()
    for copy in copies:
        copy.wait()
    first = rank * span
    sub = lax.broadcasted_iota(jnp.int32, (span, dim), 0)
    kv_sub = lax.broadcasted_iota(jnp.int32, (kv_heads, dim), 0)
    row_of = lax.broadcasted_iota(jnp.int32, (rows, span), 0)
    limit = jnp.zeros((rows, span), jnp.int32)
    for r in range(rows):
        limit = jnp.where(row_of == r, lengths[0, r] - first, limit)
        written = sub == lengths[0, r] - first
        for which in range(2):
            new_heads = new[r, which].astype(F32)
            for m in range(kv_heads):
                head = (rank // per) ^ m
                fresh = jnp.sum(
                    jnp.where(kv_sub == head, new_heads, 0.0), axis=0, keepdims=True
                )
                block = kv[r, which, head].astype(F32)
                stored_ref[r, which, m] = jnp.where(written, fresh, block).astype(BF16)
    limit_ref[...] = limit
    for copy in held:
        copy.wait()


def stage_kernel(units, weight_ref, after_ref, held_ref, sems):
    del after_ref
    copies = weight_copies(units, weight_ref, held_ref, sems)
    for copy in copies:
        copy.start()
    for copy in copies:
        copy.wait()


def append_kernel(after_ref, *refs):
    del after_ref
    parts, out_ref = refs[:-1], refs[-1]
    at = 0
    for part in parts:
        out_ref[at : at + part.shape[0]] = part[...]
        at += part.shape[0]


def packed(mixed, top, total):
    stat_sub = lax.broadcasted_iota(jnp.int32, (STAT_ROWS, LANES), 0)
    tile = jnp.zeros((STAT_ROWS, LANES), F32)
    for i, piece in enumerate(pieces(top) + pieces(total)):
        tile = jnp.where(stat_sub == i, piece, tile)
    return jnp.concatenate([mixed, tile], axis=0).astype(BF16)


def to_lanes(column):
    n = column.shape[0]
    sub = lax.broadcasted_iota(jnp.int32, (n, LANES), 0)
    lane = lax.broadcasted_iota(jnp.int32, (n, LANES), 1)
    return jnp.sum(jnp.where(lane == sub, column, 0.0), axis=0, keepdims=True)


def to_column(row, n):
    sub = lax.broadcasted_iota(jnp.int32, (n, LANES), 0)
    lane = lax.broadcasted_iota(jnp.int32, (n, LANES), 1)
    return jnp.sum(jnp.where(lane == sub, row, 0.0), axis=1, keepdims=True)


def merged(blocks):
    n = blocks[0].shape[0] - STAT_ROWS
    tops, sums = [], []
    for block in blocks:
        tile = block[n:].astype(F32)
        tops.append(tile[0:1] + tile[1:2] + tile[2:3])
        sums.append(tile[3:4] + tile[4:5] + tile[5:6])
    top = functools.reduce(jnp.maximum, tops)
    mixed, total = 0.0, 0.0
    for block, own_top, own_sum in zip(blocks, tops, sums):
        factor = jnp.exp(own_top - top)
        total = total + own_sum * factor
        mixed = mixed + block[:n].astype(F32) * to_column(factor, n)
    return mixed, top, total


def place(k, tp):
    quarter = tp // 4
    at = k % quarter * 4 + k // quarter
    return at // (tp // 2), at % (tp // 2)


def attention_kernel(stored_ref, limit_ref, after_ref, *refs):
    del after_ref
    sources, outs, (scores_ref, mixed_ref) = refs[:4], refs[4:6], refs[6:]
    quarter, rows, heads, dim = sources[0].shape
    tp = 4 * quarter
    kv_heads, span = stored_ref.shape[2:4]
    group = heads * tp // kv_heads
    per = group // heads
    scale = 1.0 / math.sqrt(dim)

    def query(k, r):
        return sources[k // quarter][k % quarter, r].astype(F32)

    for m in range(kv_heads):
        for r in range(rows):
            q = jnp.concatenate([query(m * per + i, r) for i in range(per)], axis=0).astype(BF16)
            s = lax.dot_general(
                q, stored_ref[r, 0, m], (((1,), (1,)), ((), ())), preferred_element_type=F32
            )
            scores_ref[m * group : (m + 1) * group, r, :] = s * scale

    pos = lax.broadcasted_iota(jnp.int32, (rows, span), 1)
    visible = (pos <= limit_ref[...])[None]
    scores = jnp.where(visible, scores_ref[...], -1e30)
    top = jnp.max(scores, axis=-1, keepdims=True)
    weights = jnp.where(visible, jnp.exp(scores - top), 0.0)
    total = jnp.sum(weights, axis=-1, keepdims=True)
    scores_ref[...] = weights

    for m in range(kv_heads):
        for r in range(rows):
            w = scores_ref[m * group : (m + 1) * group, r, :].astype(BF16)
            mixed_ref[m * group : (m + 1) * group, r, :] = jnp.dot(
                w, stored_ref[r, 1, m], preferred_element_type=F32
            )

    n = heads * rows
    for k in range(tp):
        own = slice(k * heads, (k + 1) * heads)
        array, at = place(k, tp)
        outs[array][at] = packed(
            mixed_ref[own].reshape(n, dim),
            to_lanes(top[own].reshape(n, 1)),
            to_lanes(total[own].reshape(n, 1)),
        )


def merge_kernel(after_ref, kept_ref, got_ref, *out_refs):
    del after_ref
    at = 0
    for out_ref in out_refs:
        for i in range(out_ref.shape[0]):
            out_ref[i] = packed(*merged([kept_ref[at], got_ref[at]]))
            at += 1


def requantized(x):
    top = jnp.max(jnp.abs(x), axis=-1, keepdims=True)
    scale = ((top + 1e-06) / 127.0).astype(BF16).astype(F32)
    return jnp.clip(jnp.floor(x / scale + 0.5), -127.0, 127.0) * scale


def project_columns(flat, weight, out_ref, i, start):
    columns = weight.shape[1]
    tile = min(512, columns)
    for c in range(0, columns, tile):
        part = jnp.dot(flat, weight[:, c : c + tile], preferred_element_type=F32)
        for b in range(0, tile, QB):
            at = start + c + b
            block = requantized(part[:, b : b + QB])
            out_ref[i, :, at : at + QB] = block.astype(out_ref.dtype)


def project_units(flat, held, places, out_ref):
    for i, (array, index) in enumerate(places):
        columns = held[array].shape[2]
        project_columns(flat, held[array].at[index], out_ref, i // 2, i % 2 * columns)


def project_away_kernel(rows, heads, places, *refs):
    sources, held, (flat_ref, out_ref) = refs[:4], refs[4:-2], refs[-2:]
    mixed, _, total = merged([source[0] for source in sources])
    attended = mixed / to_column(total, mixed.shape[0])
    flat = jnp.concatenate(
        [attended[h * rows : (h + 1) * rows] for h in range(heads)], axis=1
    ).astype(BF16)
    flat_ref[...] = flat
    project_units(flat, held, places, out_ref)


def project_own_kernel(places, units, flat_ref, weight_ref, *refs):
    held, (out_ref, late_ref, sems) = refs[:-3], refs[-3:]
    copies = weight_copies(units, weight_ref, late_ref, sems)
    for copy in copies:
        copy.start()
    flat = flat_ref[...]
    project_units(flat, held, places, out_ref)
    columns = late_ref.shape[2]
    for i, copy in enumerate(copies, len(places)):
        copy.wait()
        late = late_ref.at[i - len(places)]
        project_columns(flat, late, out_ref, i // 2, i % 2 * columns)


def split_kernel(kept_ref, got_ref, send_ref, keep_ref):
    for i in range(send_ref.shape[0]):
        send_ref[i] = (kept_ref[2 * i + 1] + got_ref[2 * i + 1].astype(F32)).astype(BF16)
        keep_ref[i] = kept_ref[2 * i] + got_ref[2 * i].astype(F32)


def pair_kernel(kept_ref, got_ref, residual_ref, even_ref, odd_ref):
    for i in range(4):
        x = kept_ref[i] + got_ref[i].astype(F32)
        if i == 0:
            x = x + residual_ref[0].astype(F32)
        if i & 1:
            odd_ref[i >> 1] = x.astype(BF16)
        else:
            even_ref[i >> 1] = x.astype(BF16)


def owner_kernel(near_ref, one_ref, two_ref, three_ref, out_ref):
    for i in range(2):
        for b in range(0, out_ref.shape[2], QB):
            at = slice(b, b + QB)
            x = near_ref[i, :, at].astype(F32) + one_ref[i, :, at].astype(F32)
            y = two_ref[1 - i, :, at].astype(F32) + three_ref[1 - i, :, at].astype(F32)
            out_ref[i, :, at] = requantized(x + y).astype(BF16)


def place_kernel(offsets, high, *refs):
    blocks, out_ref = refs[:-1], refs[-1]
    width = blocks[0].shape[2]
    rank = lax.axis_index("tp")
    for offset, block in zip(offsets, blocks):
        for i in range(2):
            start = pl.multiple_of((rank ^ offset ^ (i * high)) * width, width)
            out_ref[0, :, pl.ds(start, width)] = block[i]


def call(kernel, name, outs, args, in_specs=None, scratch=(), mib=4, cost=MIB):
    return pl.pallas_call(
        kernel,
        out_shape=outs,
        in_specs=in_specs or [VMEM_SPEC] * len(args),
        out_specs=jax.tree.map(lambda _: VMEM_SPEC, outs),
        scratch_shapes=scratch,
        compiler_params=pltpu.CompilerParams(vmem_limit_bytes=mib * MIB),
        cost_estimate=pl.CostEstimate(flops=cost, bytes_accessed=cost, transcendentals=0),
        name=name,
    )(*args)


def in_hbm(array):
    return pltpu.with_memory_space_constraint(array, pltpu.HBM)


def local(tp, sections, queries, new_kv, kv_cache, lengths, residual, out_weight):
    rows, heads, dim = queries.shape[1:]
    kv_heads, span = kv_cache.shape[3:5]
    depth, full = out_weight.shape[1:]
    width = full // tp
    half = tp // 2
    bits = tp.bit_length() - 1
    struct = jax.ShapeDtypeStruct

    def exchanged(array, k, shift=0):
        pairs = [
            (s * tp + t, ((s + shift) % sections) * tp + (t ^ k))
            for s in range(sections)
            for t in range(tp)
        ]
        return lax.ppermute(array, ("section", "tp"), pairs)

    weight = in_hbm(out_weight)
    quarter = tp // 4
    groups = [g * quarter for g in range(1, 4)]
    order = [(slot, h) for slot in (*range(1, tp, 2), *range(0, tp, 2)) for h in range(2)]
    each = tp // 8
    staged = []

    def next_units(count):
        used = sum(len(units) for units, _ in staged)
        return order[used : used + count * each]

    def held_shape(units):
        return pltpu.VMEM((len(units), depth, width // 2), BF16)

    def stage(after, count):
        units = next_units(count)
        held = call(
            functools.partial(stage_kernel, units),
            "stage",
            held_shape(units),
            (weight, after),
            in_specs=[ANY_SPEC, VMEM_SPEC],
            scratch=[pltpu.SemaphoreType.DMA((len(units),))],
            cost=2 * MIB * count,
        )
        staged.append((units, held))
        return held

    got = exchanged(queries, 1)
    units = next_units(2)
    stored, limit, have, held = call(
        functools.partial(stage_cache_kernel, tp // kv_heads, units),
        "stage_cache",
        [
            pltpu.VMEM(kv_cache.shape[1:], BF16),
            pltpu.VMEM((rows, span), jnp.int32),
            pltpu.VMEM(queries.shape, BF16),
            held_shape(units),
        ],
        (in_hbm(lengths), in_hbm(new_kv), in_hbm(kv_cache), in_hbm(queries), weight),
        in_specs=[ANY_SPEC] * 5,
        scratch=[
            pltpu.SMEM(lengths.shape, jnp.int32),
            pltpu.VMEM(new_kv.shape[1:], BF16),
            pltpu.VMEM(kv_cache.shape[1:], BF16),
            pltpu.SemaphoreType.DMA((4,)),
            pltpu.SemaphoreType.DMA((len(units),)),
        ],
        cost=8 * MIB,
    )
    staged.append((units, held))
    after = limit
    for b in range(bits - 2):
        count = 2 << b
        have = call(
            append_kernel, "append", struct((count, rows, heads, dim), BF16), (after, have, got)
        )
        after = have
        if b < bits - 3:
            got = exchanged(have, 2 << b)
    all_queries = [have, *(exchanged(have, k) for k in reversed(groups))]
    all_queries[1:] = all_queries[:0:-1]
    after = stage(have, 5)
    packed_block = (heads * rows + STAT_ROWS, dim)
    kept, send = call(
        attention_kernel,
        "attention",
        [struct((half, *packed_block), BF16)] * 2,
        (stored, limit, after, *all_queries),
        scratch=[pltpu.VMEM((heads * tp, rows, span), F32)] * 2,
        cost=8 * MIB,
    )
    got = exchanged(send, quarter // 2)
    after = stage(send, 4)
    for b in reversed(range(bits - 3)):
        kept, send = call(
            merge_kernel, "merge", [struct((4 << b, *packed_block), BF16)] * 2, (after, kept, got)
        )
        got = exchanged(send, 1 << b)
        after = send
    pending = call(
        merge_kernel, "merge", [struct((1, *packed_block), BF16)] * 4, (after, kept, got)
    )
    last = pending[3]
    pending = [pending[0], *(exchanged(block, k) for block, k in zip(pending[1:], groups))]
    stage(last, 3)

    where = {
        unit: (array, i) for array, (units, _) in enumerate(staged) for i, unit in enumerate(units)
    }
    places = [where[unit] for unit in order if unit in where]
    late = order[len(places) :]
    held = [array for _, array in staged]
    flat, away = call(
        functools.partial(project_away_kernel, rows, heads, places[:tp]),
        "project_away",
        [struct((rows, depth), BF16), struct((half, rows, width), BF16)],
        (*pending, *held),
        cost=16 * MIB,
    )
    got = exchanged(away, 1)
    kept = call(
        functools.partial(project_own_kernel, places[tp:], late),
        "project_own",
        struct((half, rows, width), F32),
        (flat, weight, *held),
        in_specs=[VMEM_SPEC, ANY_SPEC] + [VMEM_SPEC] * len(held),
        scratch=[
            pltpu.VMEM((len(late), depth, width // 2), BF16),
            pltpu.SemaphoreType.DMA((len(late),)),
        ],
        mib=14,
        cost=16 * MIB,
    )
    for b in range(1, bits - 2):
        slots = kept.shape[0] // 2
        send, kept = call(
            split_kernel,
            "split_sum",
            [struct((slots, rows, width), BF16), struct((slots, rows, width), F32)],
            (kept, got),
        )
        got = exchanged(send, 1 << b)
    even, odd = call(
        pair_kernel, "pair_sum", [struct((2, rows, width), BF16)] * 2, (kept, got, residual)
    )
    three = exchanged(odd, groups[2])
    two = exchanged(even, groups[1])
    one = exchanged(odd, groups[0])
    own = call(
        owner_kernel, "owner", struct((2, rows, width), BF16), (even, one, two, three)
    )
    high = 1 << (bits - 1)
    parts = [(k, exchanged(own, k, 1)) for k in range(high)]
    return call(
        functools.partial(place_kernel, [offset for offset, _ in parts], high),
        "placed",
        struct((1, rows, full), BF16),
        [part for _, part in parts],
    )


def solution(mesh):
    return jax.shard_map(
        functools.partial(local, mesh.shape["tp"], mesh.shape["section"]),
        mesh=mesh,
        in_specs=(
            P("section", "rep", "tp", None),
            P("section", "rep", None, None, None),
            P("section", "rep", None, None, "tp", None),
            P("section", "rep"),
            P("section", "rep", "tp"),
            P("section", "tp", None),
        ),
        out_specs=P("section", "rep", None),
        check_vma=False,
    )
```

profile of v0, /device:TPU:0, one launch (start us, length us, event | category | flops | bytes accessed | tf_op | source)
XLA Modules:
  0.0 51.7 jit_solution(11181397746324594695)
XLA Ops:
  0.0 3.0 %collective-permute-start = (bf16[1,8,8,128]{3,2,1,0:T(8,128)(2,1)}, bf16[1,8,8,128]{3,2,1,0:T(8,128)(2,1)S(1)}, u32[]{:S(2)}, u32[]{:S(2)}) collective-permute-start(bf16[1,8,8,128]{3,2,1,0:T(8,128)(2,1)} %queries_ref.1), channel_id=1, source_target_pairs={{0,1},{1,0},{2,3},{3,2},{4,5},{5,4},{6,7},{7,6},{8,9},{9,8},{10,11... | collective-permute-start | bytes 49160 | tf_op jit(solution)/shard_map/ppermute | solution.py:314
  3.0 2.9 %stage_cache.1 = (bf16[8,2,4,128,128]{4,3,2,1,0:T(8,128)(2,1)S(1)}, s32[8,128]{1,0:T(8,128)S(1)}, bf16[1,8,8,128]{3,2,1,0:T(8,128)(2,1)S(1)}, bf16[2,1024,1024]{2,1,0:T(8,128)(2,1)S(1)}) custom-call(s32[1,8]{1,0:T(1,128)} %lengths_ref.1, bf16[1,8,2,4,128]{4,3,2,1,0:T(4,128)(2,1)} %new_ref.1, bf16[1,8,2,4,128,128]{5,4,3,2,1,0:T(8,128)(2,1)} %kv_ref.1, ...), custom_call_target="tpu_custom_call" | custom-call | flops 8388608 | bytes 8388608 | tf_op jit(solution)/shard_map/stage_cache/pallas_call | solution.py:283
  5.9 3.7 %collective-permute-start.3 = (bf16[2,8,8,128]{3,2,1,0:T(8,128)(2,1)S(1)}, bf16[2,8,8,128]{3,2,1,0:T(8,128)(2,1)S(1)}, u32[]{:S(2)}, u32[]{:S(2)}) collective-permute-start(bf16[2,8,8,128]{3,2,1,0:T(8,128)(2,1)S(1)} %append.1.after_ref.refs_0_), channel_id=1, source_target_pairs={{0,6},{1,7},{2,4},{3,5},{4,2},{5,3},{6,0},{7,1},{8,14},{9,15},{10,... | collective-permute-start | bytes 98312 | tf_op jit(solution)/shard_map/ppermute | solution.py:314
  9.6 0.8 %collective-permute-start.1 = (bf16[2,8,8,128]{3,2,1,0:T(8,128)(2,1)S(1)}, bf16[2,8,8,128]{3,2,1,0:T(8,128)(2,1)S(1)}, u32[]{:S(2)}, u32[]{:S(2)}) collective-permute-start(bf16[2,8,8,128]{3,2,1,0:T(8,128)(2,1)S(1)} %append.1.after_ref.refs_0_), channel_id=1, source_target_pairs={{0,2},{1,3},{2,0},{3,1},{4,6},{5,7},{6,4},{7,5},{8,10},{9,11},{10,... | collective-permute-start | bytes 98312 | tf_op jit(solution)/shard_map/ppermute | solution.py:314
  10.4 4.1 %stage.3.after_ref.refs_5_.refs_1_ = bf16[5,1024,1024]{2,1,0:T(8,128)(2,1)S(1)} custom-call(bf16[1,1024,16384]{2,1,0:T(8,128)(2,1)} %weight_ref.9, bf16[2,8,8,128]{3,2,1,0:T(8,128)(2,1)S(1)} %append.1.after_ref.refs_0_), custom_call_target="tpu_custom_call" | custom-call | flops 10485760 | bytes 10485760 | tf_op jit(solution)/shard_map/stage/pallas_call | solution.py:283
  14.6 1.1 %attention.1 = (bf16[4,80,128]{2,1,0:T(8,128)(2,1)S(1)}, bf16[4,80,128]{2,1,0:T(8,128)(2,1)S(1)}) custom-call(bf16[8,2,4,128,128]{4,3,2,1,0:T(8,128)(2,1)S(1)} %get-tuple-element.19.stored_ref, s32[8,128]{1,0:T(8,128)S(1)} %get-tuple-element.20.after_ref.limit_ref, bf16[5,1024,1024]{2,1,0:T(8,128)(2,1)S(1)} %stage.3.after_ref.refs_5_.refs_1_, ...), custom_call_target="tpu_custom_call" | custom-call | flops 8388608 | bytes 8388608 | tf_op jit(solution)/shard_map/attention/pallas_call | solution.py:283
  15.7 1.0 %collective-permute-start.4 = (bf16[4,80,128]{2,1,0:T(8,128)(2,1)S(1)}, bf16[4,80,128]{2,1,0:T(8,128)(2,1)S(1)}, u32[]{:S(2)}, u32[]{:S(2)}) collective-permute-start(bf16[4,80,128]{2,1,0:T(8,128)(2,1)S(1)} %get-tuple-element.22.after_ref), channel_id=1, source_target_pairs={{0,1},{1,0},{2,3},{3,2},{4,5},{5,4},{6,7},{7,6},{8,9},{9,8},{10,11... | collective-permute-start | bytes 245768 | tf_op jit(solution)/shard_map/ppermute | solution.py:314
  16.7 3.5 %stage.4.after_ref.refs_6_.refs_2_ = bf16[4,1024,1024]{2,1,0:T(8,128)(2,1)S(1)} custom-call(bf16[1,1024,16384]{2,1,0:T(8,128)(2,1)} %weight_ref.9, bf16[4,80,128]{2,1,0:T(8,128)(2,1)S(1)} %get-tuple-element.22.after_ref), custom_call_target="tpu_custom_call" | custom-call | flops 8388608 | bytes 8388608 | tf_op jit(solution)/shard_map/stage/pallas_call | solution.py:283
  20.4 1.3 %collective-permute-start.5 = (bf16[1,80,128]{2,1,0:T(8,128)(2,1)S(1)}, bf16[1,80,128]{2,1,0:T(8,128)(2,1)S(1)}, u32[]{:S(2)}, u32[]{:S(2)}) collective-permute-start(bf16[1,80,128]{2,1,0:T(8,128)(2,1)S(1)} %get-tuple-element.25), channel_id=1, source_target_pairs={{0,2},{1,3},{2,0},{3,1},{4,6},{5,7},{6,4},{7,5},{8,10},{9,11},{10,... | collective-permute-start | bytes 61448 | tf_op jit(solution)/shard_map/ppermute | solution.py:314
  21.7 2.9 %collective-permute-start.6 = (bf16[1,80,128]{2,1,0:T(8,128)(2,1)S(1)}, bf16[1,80,128]{2,1,0:T(8,128)(2,1)S(1)}, u32[]{:S(2)}, u32[]{:S(2)}) collective-permute-start(bf16[1,80,128]{2,1,0:T(8,128)(2,1)S(1)} %get-tuple-element.26), channel_id=1, source_target_pairs={{0,4},{1,5},{2,6},{3,7},{4,0},{5,1},{6,2},{7,3},{8,12},{9,13},{10,... | collective-permute-start | bytes 61448 | tf_op jit(solution)/shard_map/ppermute | solution.py:314
  24.8 2.9 %stage.5.refs_7_.refs_3_ = bf16[3,1024,1024]{2,1,0:T(8,128)(2,1)S(1)} custom-call(bf16[1,1024,16384]{2,1,0:T(8,128)(2,1)} %weight_ref.9, bf16[1,80,128]{2,1,0:T(8,128)(2,1)S(1)} %get-tuple-element.27.after_ref), custom_call_target="tpu_custom_call" | custom-call | flops 6291456 | bytes 6291456 | tf_op jit(solution)/shard_map/stage/pallas_call | solution.py:283
  27.8 2.4 %collective-permute-done.7.refs_3_ = bf16[1,80,128]{2,1,0:T(8,128)(2,1)S(1)} collective-permute-done((bf16[1,80,128]{2,1,0:T(8,128)(2,1)S(1)}, bf16[1,80,128]{2,1,0:T(8,128)(2,1)S(1)}, u32[]{:S(2)}, u32[]{:S(2)}) %collective-permute-start.7) | collective-permute-done | bytes 20512 | tf_op jit(solution)/shard_map/ppermute | solution.py:314
  30.2 2.5 %project_away.1 = (bf16[8,1024]{1,0:T(8,128)(2,1)S(1)}, bf16[4,8,2048]{2,1,0:T(8,128)(2,1)S(1)}) custom-call(bf16[1,80,128]{2,1,0:T(8,128)(2,1)S(1)} %get-tuple-element.24.refs_0_, bf16[1,80,128]{2,1,0:T(8,128)(2,1)S(1)} %collective-permute-done.5.refs_1_, bf16[1,80,128]{2,1,0:T(8,128)(2,1)S(1)} %collective-permute-done.6.refs_2_, ...), custom_call_target="tpu_custom_call" | custom-call | flops 16777216 | bytes 16777216 | tf_op jit(solution)/shard_map/project_away/pallas_call | solution.py:283
  32.7 1.2 %collective-permute-start.8 = (bf16[4,8,2048]{2,1,0:T(8,128)(2,1)S(1)}, bf16[4,8,2048]{2,1,0:T(8,128)(2,1)S(1)}, u32[]{:S(2)}, u32[]{:S(2)}) collective-permute-start(bf16[4,8,2048]{2,1,0:T(8,128)(2,1)S(1)} %get-tuple-element.30), channel_id=1, source_target_pairs={{0,1},{1,0},{2,3},{3,2},{4,5},{5,4},{6,7},{7,6},{8,9},{9,8},{10,11... | collective-permute-start | bytes 393224 | tf_op jit(solution)/shard_map/ppermute | solution.py:314
  33.8 3.9 %project_own.1.kept_ref = f32[4,8,2048]{2,1,0:T(8,128)S(1)} custom-call(bf16[8,1024]{1,0:T(8,128)(2,1)S(1)} %get-tuple-element.29.flat_ref, bf16[1,1024,16384]{2,1,0:T(8,128)(2,1)} %weight_ref.9, bf16[2,1024,1024]{2,1,0:T(8,128)(2,1)S(1)} %get-tuple-element.28.refs_4_.refs_0_, bf16[5,1024,1024]{2,1,0:T(8,128)(2,1)S(1)} %stage.3.after_ref.refs_5_.refs_1_, ...), custom_call_target="tpu_custom_call" | custom-call | flops 16777216 | bytes 16777216 | tf_op jit(solution)/shard_map/project_own/pallas_call | solution.py:283
  37.9 1.2 %collective-permute-start.11 = (bf16[2,8,2048]{2,1,0:T(8,128)(2,1)S(1)}, bf16[2,8,2048]{2,1,0:T(8,128)(2,1)S(1)}, u32[]{:S(2)}, u32[]{:S(2)}) collective-permute-start(bf16[2,8,2048]{2,1,0:T(8,128)(2,1)S(1)} %get-tuple-element.32), channel_id=1, source_target_pairs={{0,6},{1,7},{2,4},{3,5},{4,2},{5,3},{6,0},{7,1},{8,14},{9,15},{10,... | collective-permute-start | bytes 196616 | tf_op jit(solution)/shard_map/ppermute | solution.py:314
  39.1 2.2 %collective-permute-start.9 = (bf16[2,8,2048]{2,1,0:T(8,128)(2,1)S(1)}, bf16[2,8,2048]{2,1,0:T(8,128)(2,1)S(1)}, u32[]{:S(2)}, u32[]{:S(2)}) collective-permute-start(bf16[2,8,2048]{2,1,0:T(8,128)(2,1)S(1)} %get-tuple-element.32), channel_id=1, source_target_pairs={{0,2},{1,3},{2,0},{3,1},{4,6},{5,7},{6,4},{7,5},{8,10},{9,11},{10,... | collective-permute-start | bytes 196616 | tf_op jit(solution)/shard_map/ppermute | solution.py:314
  41.3 1.7 %collective-permute-done.10.two_ref = bf16[2,8,2048]{2,1,0:T(8,128)(2,1)S(1)} collective-permute-done((bf16[2,8,2048]{2,1,0:T(8,128)(2,1)S(1)}, bf16[2,8,2048]{2,1,0:T(8,128)(2,1)S(1)}, u32[]{:S(2)}, u32[]{:S(2)}) %collective-permute-start.10) | collective-permute-done | bytes 65568 | tf_op jit(solution)/shard_map/ppermute | solution.py:314
  43.0 1.1 %collective-permute-done.11.three_ref = bf16[2,8,2048]{2,1,0:T(8,128)(2,1)S(1)} collective-permute-done((bf16[2,8,2048]{2,1,0:T(8,128)(2,1)S(1)}, bf16[2,8,2048]{2,1,0:T(8,128)(2,1)S(1)}, u32[]{:S(2)}, u32[]{:S(2)}) %collective-permute-start.11) | collective-permute-done | bytes 65568 | tf_op jit(solution)/shard_map/ppermute | solution.py:314
  44.6 2.2 %collective-permute-start.14 = (bf16[2,8,2048]{2,1,0:T(8,128)(2,1)S(1)}, bf16[2,8,2048]{2,1,0:T(8,128)(2,1)S(1)}, u32[]{:S(2)}, u32[]{:S(2)}) collective-permute-start(bf16[2,8,2048]{2,1,0:T(8,128)(2,1)S(1)} %owner.1), channel_id=1, source_target_pairs={{0,10},{1,11},{2,8},{3,9},{4,14},{5,15},{6,12},{7,13},{8,2},{9,3},... | collective-permute-start | bytes 196616 | tf_op jit(solution)/shard_map/ppermute | solution.py:314
  47.0 1.0 %collective-permute-start.12 = (bf16[2,8,2048]{2,1,0:T(8,128)(2,1)S(1)}, bf16[2,8,2048]{2,1,0:T(8,128)(2,1)S(1)}, u32[]{:S(2)}, u32[]{:S(2)}) collective-permute-start(bf16[2,8,2048]{2,1,0:T(8,128)(2,1)S(1)} %owner.1), channel_id=1, source_target_pairs={{0,8},{1,9},{2,10},{3,11},{4,12},{5,13},{6,14},{7,15},{8,0},{9,1},... | collective-permute-start | bytes 196616 | tf_op jit(solution)/shard_map/ppermute | solution.py:314
  47.9 1.3 %collective-permute-done.15.refs_3_ = bf16[2,8,2048]{2,1,0:T(8,128)(2,1)S(1)} collective-permute-done((bf16[2,8,2048]{2,1,0:T(8,128)(2,1)S(1)}, bf16[2,8,2048]{2,1,0:T(8,128)(2,1)S(1)}, u32[]{:S(2)}, u32[]{:S(2)}) %collective-permute-start.15) | collective-permute-done | bytes 65568 | tf_op jit(solution)/shard_map/ppermute | solution.py:314
  49.5 1.5 %collective-permute-done.13.refs_1_ = bf16[2,8,2048]{2,1,0:T(8,128)(2,1)S(1)} collective-permute-done((bf16[2,8,2048]{2,1,0:T(8,128)(2,1)S(1)}, bf16[2,8,2048]{2,1,0:T(8,128)(2,1)S(1)}, u32[]{:S(2)}, u32[]{:S(2)}) %collective-permute-start.13) | collective-permute-done | bytes 65568 | tf_op jit(solution)/shard_map/ppermute | solution.py:314
  51.0 0.7 %placed.1 = bf16[1,8,16384]{2,1,0:T(8,128)(2,1)} custom-call(bf16[2,8,2048]{2,1,0:T(8,128)(2,1)S(1)} %collective-permute-done.12.refs_0_, bf16[2,8,2048]{2,1,0:T(8,128)(2,1)S(1)} %collective-permute-done.13.refs_1_, bf16[2,8,2048]{2,1,0:T(8,128)(2,1)S(1)} %collective-permute-done.14.refs_2_, bf16[2,8,2048]{2,1,0:T(8,128)(2,1)S(1)} %collective-permute-done.15.refs_3_), custom_call_target="tpu_custom_call" | custom-call | flops 1048576 | bytes 1048576 | tf_op jit(solution)/shard_map/placed/pallas_call | solution.py:283
  (22 shorter events, 1.4 us)
Async XLA Ops:
  0.0 5.9 %collective-permute-start = (bf16[1,8,8,128]{3,2,1,0:T(8,128)(2,1)}, bf16[1,8,8,128]{3,2,1,0:T(8,128)(2,1)S(1)}, u32[]{:S(2)}, u32[]{:S(2)}) collective-permute-start(bf16[1,8,8,128]{3,2,1,0:T(8,128)(2,1)} %queries_ref.1), channel_id=1, source_target_pairs={{0,1},{1,0},{2,3},{3,2},{4,5},{5,4},{6,7},{7,6},{8,9},{9,8},{10,11... | collective-permute-start | bytes 49160 | tf_op jit(solution)/shard_map/ppermute | solution.py:314
  5.9 8.6 %collective-permute-start.3 = (bf16[2,8,8,128]{3,2,1,0:T(8,128)(2,1)S(1)}, bf16[2,8,8,128]{3,2,1,0:T(8,128)(2,1)S(1)}, u32[]{:S(2)}, u32[]{:S(2)}) collective-permute-start(bf16[2,8,8,128]{3,2,1,0:T(8,128)(2,1)S(1)} %append.1.after_ref.refs_0_), channel_id=1, source_target_pairs={{0,6},{1,7},{2,4},{3,5},{4,2},{5,3},{6,0},{7,1},{8,14},{9,15},{10,... | collective-permute-start | bytes 98312 | tf_op jit(solution)/shard_map/ppermute | solution.py:314
  9.6 4.9 %collective-permute-start.2 = (bf16[2,8,8,128]{3,2,1,0:T(8,128)(2,1)S(1)}, bf16[2,8,8,128]{3,2,1,0:T(8,128)(2,1)S(1)}, u32[]{:S(2)}, u32[]{:S(2)}) collective-permute-start(bf16[2,8,8,128]{3,2,1,0:T(8,128)(2,1)S(1)} %append.1.after_ref.refs_0_), channel_id=1, source_target_pairs={{0,4},{1,5},{2,6},{3,7},{4,0},{5,1},{6,2},{7,3},{8,12},{9,13},{10,... | collective-permute-start | bytes 98312 | tf_op jit(solution)/shard_map/ppermute | solution.py:314
  9.6 5.0 %collective-permute-start.1 = (bf16[2,8,8,128]{3,2,1,0:T(8,128)(2,1)S(1)}, bf16[2,8,8,128]{3,2,1,0:T(8,128)(2,1)S(1)}, u32[]{:S(2)}, u32[]{:S(2)}) collective-permute-start(bf16[2,8,8,128]{3,2,1,0:T(8,128)(2,1)S(1)} %append.1.after_ref.refs_0_), channel_id=1, source_target_pairs={{0,2},{1,3},{2,0},{3,1},{4,6},{5,7},{6,4},{7,5},{8,10},{9,11},{10,... | collective-permute-start | bytes 98312 | tf_op jit(solution)/shard_map/ppermute | solution.py:314
  15.7 4.5 %collective-permute-start.4 = (bf16[4,80,128]{2,1,0:T(8,128)(2,1)S(1)}, bf16[4,80,128]{2,1,0:T(8,128)(2,1)S(1)}, u32[]{:S(2)}, u32[]{:S(2)}) collective-permute-start(bf16[4,80,128]{2,1,0:T(8,128)(2,1)S(1)} %get-tuple-element.22.after_ref), channel_id=1, source_target_pairs={{0,1},{1,0},{2,3},{3,2},{4,5},{5,4},{6,7},{7,6},{8,9},{9,8},{10,11... | collective-permute-start | bytes 245768 | tf_op jit(solution)/shard_map/ppermute | solution.py:314
  20.4 7.4 %collective-permute-start.5 = (bf16[1,80,128]{2,1,0:T(8,128)(2,1)S(1)}, bf16[1,80,128]{2,1,0:T(8,128)(2,1)S(1)}, u32[]{:S(2)}, u32[]{:S(2)}) collective-permute-start(bf16[1,80,128]{2,1,0:T(8,128)(2,1)S(1)} %get-tuple-element.25), channel_id=1, source_target_pairs={{0,2},{1,3},{2,0},{3,1},{4,6},{5,7},{6,4},{7,5},{8,10},{9,11},{10,... | collective-permute-start | bytes 61448 | tf_op jit(solution)/shard_map/ppermute | solution.py:314
  21.7 6.1 %collective-permute-start.6 = (bf16[1,80,128]{2,1,0:T(8,128)(2,1)S(1)}, bf16[1,80,128]{2,1,0:T(8,128)(2,1)S(1)}, u32[]{:S(2)}, u32[]{:S(2)}) collective-permute-start(bf16[1,80,128]{2,1,0:T(8,128)(2,1)S(1)} %get-tuple-element.26), channel_id=1, source_target_pairs={{0,4},{1,5},{2,6},{3,7},{4,0},{5,1},{6,2},{7,3},{8,12},{9,13},{10,... | collective-permute-start | bytes 61448 | tf_op jit(solution)/shard_map/ppermute | solution.py:314
  24.6 5.6 %collective-permute-start.7 = (bf16[1,80,128]{2,1,0:T(8,128)(2,1)S(1)}, bf16[1,80,128]{2,1,0:T(8,128)(2,1)S(1)}, u32[]{:S(2)}, u32[]{:S(2)}) collective-permute-start(bf16[1,80,128]{2,1,0:T(8,128)(2,1)S(1)} %get-tuple-element.27.after_ref), channel_id=1, source_target_pairs={{0,6},{1,7},{2,4},{3,5},{4,2},{5,3},{6,0},{7,1},{8,14},{9,15},{10,... | collective-permute-start | bytes 61448 | tf_op jit(solution)/shard_map/ppermute | solution.py:314
  32.7 5.1 %collective-permute-start.8 = (bf16[4,8,2048]{2,1,0:T(8,128)(2,1)S(1)}, bf16[4,8,2048]{2,1,0:T(8,128)(2,1)S(1)}, u32[]{:S(2)}, u32[]{:S(2)}) collective-permute-start(bf16[4,8,2048]{2,1,0:T(8,128)(2,1)S(1)} %get-tuple-element.30), channel_id=1, source_target_pairs={{0,1},{1,0},{2,3},{3,2},{4,5},{5,4},{6,7},{7,6},{8,9},{9,8},{10,11... | collective-permute-start | bytes 393224 | tf_op jit(solution)/shard_map/ppermute | solution.py:314
  33.8 3.9 %copy-start = (bf16[1,8,2048]{2,1,0:T(8,128)(2,1)S(1)}, bf16[1,8,2048]{2,1,0:T(8,128)(2,1)}, u32[]{:S(2)}) copy-start(bf16[1,8,2048]{2,1,0:T(8,128)(2,1)} %residual_ref.1) | copy-start | bytes 98308
  37.8 5.2 %collective-permute-start.10 = (bf16[2,8,2048]{2,1,0:T(8,128)(2,1)S(1)}, bf16[2,8,2048]{2,1,0:T(8,128)(2,1)S(1)}, u32[]{:S(2)}, u32[]{:S(2)}) collective-permute-start(bf16[2,8,2048]{2,1,0:T(8,128)(2,1)S(1)} %get-tuple-element.31.near_ref), channel_id=1, source_target_pairs={{0,4},{1,5},{2,6},{3,7},{4,0},{5,1},{6,2},{7,3},{8,12},{9,13},{10,... | collective-permute-start | bytes 196616 | tf_op jit(solution)/shard_map/ppermute | solution.py:314
  37.9 6.3 %collective-permute-start.11 = (bf16[2,8,2048]{2,1,0:T(8,128)(2,1)S(1)}, bf16[2,8,2048]{2,1,0:T(8,128)(2,1)S(1)}, u32[]{:S(2)}, u32[]{:S(2)}) collective-permute-start(bf16[2,8,2048]{2,1,0:T(8,128)(2,1)S(1)} %get-tuple-element.32), channel_id=1, source_target_pairs={{0,6},{1,7},{2,4},{3,5},{4,2},{5,3},{6,0},{7,1},{8,14},{9,15},{10,... | collective-permute-start | bytes 196616 | tf_op jit(solution)/shard_map/ppermute | solution.py:314
  39.1 5.3 %collective-permute-start.9 = (bf16[2,8,2048]{2,1,0:T(8,128)(2,1)S(1)}, bf16[2,8,2048]{2,1,0:T(8,128)(2,1)S(1)}, u32[]{:S(2)}, u32[]{:S(2)}) collective-permute-start(bf16[2,8,2048]{2,1,0:T(8,128)(2,1)S(1)} %get-tuple-element.32), channel_id=1, source_target_pairs={{0,2},{1,3},{2,0},{3,1},{4,6},{5,7},{6,4},{7,5},{8,10},{9,11},{10,... | collective-permute-start | bytes 196616 | tf_op jit(solution)/shard_map/ppermute | solution.py:314
  44.6 4.7 %collective-permute-start.15 = (bf16[2,8,2048]{2,1,0:T(8,128)(2,1)S(1)}, bf16[2,8,2048]{2,1,0:T(8,128)(2,1)S(1)}, u32[]{:S(2)}, u32[]{:S(2)}) collective-permute-start(bf16[2,8,2048]{2,1,0:T(8,128)(2,1)S(1)} %owner.1), channel_id=1, source_target_pairs={{0,11},{1,10},{2,9},{3,8},{4,15},{5,14},{6,13},{7,12},{8,3},{9,2},... | collective-permute-start | bytes 196616 | tf_op jit(solution)/shard_map/ppermute | solution.py:314
  44.6 4.9 %collective-permute-start.14 = (bf16[2,8,2048]{2,1,0:T(8,128)(2,1)S(1)}, bf16[2,8,2048]{2,1,0:T(8,128)(2,1)S(1)}, u32[]{:S(2)}, u32[]{:S(2)}) collective-permute-start(bf16[2,8,2048]{2,1,0:T(8,128)(2,1)S(1)} %owner.1), channel_id=1, source_target_pairs={{0,10},{1,11},{2,8},{3,9},{4,14},{5,15},{6,12},{7,13},{8,2},{9,3},... | collective-permute-start | bytes 196616 | tf_op jit(solution)/shard_map/ppermute | solution.py:314
  46.9 4.1 %collective-permute-start.13 = (bf16[2,8,2048]{2,1,0:T(8,128)(2,1)S(1)}, bf16[2,8,2048]{2,1,0:T(8,128)(2,1)S(1)}, u32[]{:S(2)}, u32[]{:S(2)}) collective-permute-start(bf16[2,8,2048]{2,1,0:T(8,128)(2,1)S(1)} %owner.1), channel_id=1, source_target_pairs={{0,9},{1,8},{2,11},{3,10},{4,13},{5,12},{6,15},{7,14},{8,1},{9,0},... | collective-permute-start | bytes 196616 | tf_op jit(solution)/shard_map/ppermute | solution.py:314
  47.0 4.0 %collective-permute-start.12 = (bf16[2,8,2048]{2,1,0:T(8,128)(2,1)S(1)}, bf16[2,8,2048]{2,1,0:T(8,128)(2,1)S(1)}, u32[]{:S(2)}, u32[]{:S(2)}) collective-permute-start(bf16[2,8,2048]{2,1,0:T(8,128)(2,1)S(1)} %owner.1), channel_id=1, source_target_pairs={{0,8},{1,9},{2,10},{3,11},{4,12},{5,13},{6,14},{7,15},{8,0},{9,1},... | collective-permute-start | bytes 196616 | tf_op jit(solution)/shard_map/ppermute | solution.py:314
where the time goes:
time: 51.9 us; the launch traced here: 51.7 us
  Pallas kernels  22 us (42%)
  starting transfers between devices  21 us (40%)
  waiting for transfers between devices  8.59 us (17%)
    pallas_call x12, Pallas kernels, call(): pl.pallas_call(kernel, out_shape=outs, in_specs=in_specs or [VMEM_SPEC] *...  22 us
    ppermute x16, starting transfers between devices, exchanged(): return lax.ppermute(array, ('section', 'tp'), pairs)  21 us
    ppermute x16, waiting for transfers between devices, exchanged(): return lax.ppermute(array, ('section', 'tp'), pairs)  8.59 us
  transfers between devices with their start and end apart: 16, of which 7 were waited for; matrix products, arithmetic and copies ran while one was open for 0% of the time, Pallas kernels for 34%

commit v1 on v0

--- a/solution.py
+++ b/solution.py
@@ -135,7 +135,8 @@
 
 def place(k, tp):
     quarter = tp // 4
-    at = k % quarter * 4 + k // quarter
+    top = k // quarter
+    at = k % quarter * 4 + top % 2 * 2 + top // 2
     return at // (tp // 2), at % (tp // 2)
 
 
@@ -218,9 +219,9 @@
         project_columns(flat, held[array].at[index], out_ref, i // 2, i % 2 * columns)
 
 
-def project_away_kernel(rows, heads, places, *refs):
-    sources, held, (flat_ref, out_ref) = refs[:4], refs[4:-2], refs[-2:]
-    mixed, _, total = merged([source[0] for source in sources])
+def project_away_kernel(rows, heads, places, kept_ref, got_ref, *refs):
+    held, (flat_ref, out_ref) = refs[:-2], refs[-2:]
+    mixed, _, total = merged([kept_ref[0], got_ref[0]])
     attended = mixed / to_column(total, mixed.shape[0])
     flat = jnp.concatenate(
         [attended[h * rows : (h + 1) * rows] for h in range(heads)], axis=1
@@ -375,7 +376,7 @@
             got = exchanged(have, 2 << b)
     all_queries = [have, *(exchanged(have, k) for k in reversed(groups))]
     all_queries[1:] = all_queries[:0:-1]
-    after = stage(have, 5)
+    after = stage(have, 2)
     packed_block = (heads * rows + STAT_ROWS, dim)
     kept, send = call(
         attention_kernel,
@@ -387,18 +388,14 @@
     )
     got = exchanged(send, quarter // 2)
     after = stage(send, 4)
-    for b in reversed(range(bits - 3)):
+    count = half
+    for k in [1 << b for b in reversed(range(bits - 3))] + groups[:2]:
+        count //= 2
         kept, send = call(
-            merge_kernel, "merge", [struct((4 << b, *packed_block), BF16)] * 2, (after, kept, got)
-        )
-        got = exchanged(send, 1 << b)
-        after = send
-    pending = call(
-        merge_kernel, "merge", [struct((1, *packed_block), BF16)] * 4, (after, kept, got)
-    )
-    last = pending[3]
-    pending = [pending[0], *(exchanged(block, k) for block, k in zip(pending[1:], groups))]
-    stage(last, 3)
+            merge_kernel, "merge", [struct((count, *packed_block), BF16)] * 2, (after, kept, got)
+        )
+        got = exchanged(send, k)
+        after = stage(send, 3) if k in groups else send
 
     where = {
         unit: (array, i) for array, (units, _) in enumerate(staged) for i, unit in enumerate(units)
@@ -410,7 +407,7 @@
         functools.partial(project_away_kernel, rows, heads, places[:tp]),
         "project_away",
         [struct((rows, depth), BF16), struct((half, rows, width), BF16)],
-        (*pending, *held),
+        (kept, got, *held),
         cost=16 * MIB,
     )
     got = exchanged(away, 1)

time: 51.9 us -> 52.7 us (1.015)
  starting transfers between devices: 21 us -> 18.7 us
  waiting for transfers between devices: 8.59 us -> 10.6 us
  Pallas kernels: 22 us -> 23.1 us
    ppermute x16 -> x15, starting transfers between devices: 21 us -> 18.7 us  [exchanged(): return lax.ppermute(array, ('section', 'tp'), pairs)]
    ppermute x16 -> x15, waiting for transfers between devices: 8.59 us -> 10.6 us  [exchanged(): return lax.ppermute(array, ('section', 'tp'), pairs)]
    pallas_call x12 -> x14, Pallas kernels: 22 us -> 23.1 us  [call(): pl.pallas_call(kernel, out_shape=outs, in_specs=in_specs or [VMEM_SPEC] *...]
  transfers between devices with their start and end apart: 16 -> 15, of which waited for: 7 -> 9; matrix products, arithmetic and copies ran while one was open for 0% -> 0% of each run, Pallas kernels for 34% -> 35%
where the time goes in v1:
time: 52.7 us; the launch traced here: 52.6 us
  Pallas kernels  23.1 us (44%)
  starting transfers between devices  18.7 us (35%)
  waiting for transfers between devices  10.6 us (20%)
    pallas_call x14, Pallas kernels, call(): pl.pallas_call(kernel, out_shape=outs, in_specs=in_specs or [VMEM_SPEC] *...  23.1 us
    ppermute x15, starting transfers between devices, exchanged(): return lax.ppermute(array, ('section', 'tp'), pairs)  18.7 us
    ppermute x15, waiting for transfers between devices, exchanged(): return lax.ppermute(array, ('section', 'tp'), pairs)  10.6 us
  transfers between devices with their start and end apart: 15, of which 9 were waited for; matrix products, arithmetic and copies ran while one was open for 0% of the time, Pallas kernels for 35%

profile of v1, /device:TPU:0, one launch (start us, length us, event | category | flops | bytes accessed | tf_op | source)
XLA Modules:
  0.0 52.6 jit_solution(8406914081316136040)
XLA Ops:
  0.0 3.0 %collective-permute-start = (bf16[1,8,8,128]{3,2,1,0:T(8,128)(2,1)}, bf16[1,8,8,128]{3,2,1,0:T(8,128)(2,1)S(1)}, u32[]{:S(2)}, u32[]{:S(2)}) collective-permute-start(bf16[1,8,8,128]{3,2,1,0:T(8,128)(2,1)} %queries_ref.1), channel_id=1, source_target_pairs={{0,1},{1,0},{2,3},{3,2},{4,5},{5,4},{6,7},{7,6},{8,9},{9,8},{10,11... | collective-permute-start | bytes 49160 | tf_op jit(solution)/shard_map/ppermute | solution.py:315
  3.0 2.9 %stage_cache.1 = (bf16[8,2,4,128,128]{4,3,2,1,0:T(8,128)(2,1)S(1)}, s32[8,128]{1,0:T(8,128)S(1)}, bf16[1,8,8,128]{3,2,1,0:T(8,128)(2,1)S(1)}, bf16[2,1024,1024]{2,1,0:T(8,128)(2,1)S(1)}) custom-call(s32[1,8]{1,0:T(1,128)} %lengths_ref.1, bf16[1,8,2,4,128]{4,3,2,1,0:T(4,128)(2,1)} %new_ref.1, bf16[1,8,2,4,128,128]{5,4,3,2,1,0:T(8,128)(2,1)} %kv_ref.1, ...), custom_call_target="tpu_custom_call" | custom-call | flops 8388608 | bytes 8388608 | tf_op jit(solution)/shard_map/stage_cache/pallas_call | solution.py:284
  5.9 3.7 %collective-permute-start.3 = (bf16[2,8,8,128]{3,2,1,0:T(8,128)(2,1)S(1)}, bf16[2,8,8,128]{3,2,1,0:T(8,128)(2,1)S(1)}, u32[]{:S(2)}, u32[]{:S(2)}) collective-permute-start(bf16[2,8,8,128]{3,2,1,0:T(8,128)(2,1)S(1)} %append.1.after_ref.refs_0_), channel_id=1, source_target_pairs={{0,6},{1,7},{2,4},{3,5},{4,2},{5,3},{6,0},{7,1},{8,14},{9,15},{10,... | collective-permute-start | bytes 98312 | tf_op jit(solution)/shard_map/ppermute | solution.py:315
  9.6 0.8 %collective-permute-start.1 = (bf16[2,8,8,128]{3,2,1,0:T(8,128)(2,1)S(1)}, bf16[2,8,8,128]{3,2,1,0:T(8,128)(2,1)S(1)}, u32[]{:S(2)}, u32[]{:S(2)}) collective-permute-start(bf16[2,8,8,128]{3,2,1,0:T(8,128)(2,1)S(1)} %append.1.after_ref.refs_0_), channel_id=1, source_target_pairs={{0,2},{1,3},{2,0},{3,1},{4,6},{5,7},{6,4},{7,5},{8,10},{9,11},{10,... | collective-permute-start | bytes 98312 | tf_op jit(solution)/shard_map/ppermute | solution.py:315
  10.4 2.2 %stage.4.after_ref.refs_1_ = bf16[2,1024,1024]{2,1,0:T(8,128)(2,1)S(1)} custom-call(bf16[1,1024,16384]{2,1,0:T(8,128)(2,1)} %weight_ref.11, bf16[2,8,8,128]{3,2,1,0:T(8,128)(2,1)S(1)} %append.1.after_ref.refs_0_), custom_call_target="tpu_custom_call" | custom-call | flops 4194304 | bytes 4194304 | tf_op jit(solution)/shard_map/stage/pallas_call | solution.py:284
  12.7 1.8 %collective-permute-done.2.refs_2_ = bf16[2,8,8,128]{3,2,1,0:T(8,128)(2,1)S(1)} collective-permute-done((bf16[2,8,8,128]{3,2,1,0:T(8,128)(2,1)S(1)}, bf16[2,8,8,128]{3,2,1,0:T(8,128)(2,1)S(1)}, u32[]{:S(2)}, u32[]{:S(2)}) %collective-permute-start.2) | collective-permute-done | bytes 32800 | tf_op jit(solution)/shard_map/ppermute | solution.py:315
  14.4 1.1 %attention.1 = (bf16[4,80,128]{2,1,0:T(8,128)(2,1)S(1)}, bf16[4,80,128]{2,1,0:T(8,128)(2,1)S(1)}) custom-call(bf16[8,2,4,128,128]{4,3,2,1,0:T(8,128)(2,1)S(1)} %get-tuple-element.19.stored_ref, s32[8,128]{1,0:T(8,128)S(1)} %get-tuple-element.20.after_ref.limit_ref, bf16[2,1024,1024]{2,1,0:T(8,128)(2,1)S(1)} %stage.4.after_ref.refs_1_, ...), custom_call_target="tpu_custom_call" | custom-call | flops 8388608 | bytes 8388608 | tf_op jit(solution)/shard_map/attention/pallas_call | solution.py:284
  15.5 1.0 %collective-permute-start.4 = (bf16[4,80,128]{2,1,0:T(8,128)(2,1)S(1)}, bf16[4,80,128]{2,1,0:T(8,128)(2,1)S(1)}, u32[]{:S(2)}, u32[]{:S(2)}) collective-permute-start(bf16[4,80,128]{2,1,0:T(8,128)(2,1)S(1)} %get-tuple-element.22.after_ref), channel_id=1, source_target_pairs={{0,1},{1,0},{2,3},{3,2},{4,5},{5,4},{6,7},{7,6},{8,9},{9,8},{10,11... | collective-permute-start | bytes 245768 | tf_op jit(solution)/shard_map/ppermute | solution.py:315
  16.5 3.5 %stage.5.after_ref.refs_2_ = bf16[4,1024,1024]{2,1,0:T(8,128)(2,1)S(1)} custom-call(bf16[1,1024,16384]{2,1,0:T(8,128)(2,1)} %weight_ref.11, bf16[4,80,128]{2,1,0:T(8,128)(2,1)S(1)} %get-tuple-element.22.after_ref), custom_call_target="tpu_custom_call" | custom-call | flops 8388608 | bytes 8388608 | tf_op jit(solution)/shard_map/stage/pallas_call | solution.py:284
  20.3 2.9 %stage.6.after_ref.refs_3_ = bf16[3,1024,1024]{2,1,0:T(8,128)(2,1)S(1)} custom-call(bf16[1,1024,16384]{2,1,0:T(8,128)(2,1)} %weight_ref.11, bf16[2,80,128]{2,1,0:T(8,128)(2,1)S(1)} %get-tuple-element.24.after_ref), custom_call_target="tpu_custom_call" | custom-call | flops 6291456 | bytes 6291456 | tf_op jit(solution)/shard_map/stage/pallas_call | solution.py:284
  23.2 1.1 %collective-permute-done.5.got_ref = bf16[2,80,128]{2,1,0:T(8,128)(2,1)S(1)} collective-permute-done((bf16[2,80,128]{2,1,0:T(8,128)(2,1)S(1)}, bf16[2,80,128]{2,1,0:T(8,128)(2,1)S(1)}, u32[]{:S(2)}, u32[]{:S(2)}) %collective-permute-start.5) | collective-permute-done | bytes 40992 | tf_op jit(solution)/shard_map/ppermute | solution.py:315
  24.4 2.3 %collective-permute-start.6 = (bf16[1,80,128]{2,1,0:T(8,128)(2,1)S(1)}, bf16[1,80,128]{2,1,0:T(8,128)(2,1)S(1)}, u32[]{:S(2)}, u32[]{:S(2)}) collective-permute-start(bf16[1,80,128]{2,1,0:T(8,128)(2,1)S(1)} %get-tuple-element.27.after_ref), channel_id=1, source_target_pairs={{0,4},{1,5},{2,6},{3,7},{4,0},{5,1},{6,2},{7,3},{8,12},{9,13},{10,... | collective-permute-start | bytes 61448 | tf_op jit(solution)/shard_map/ppermute | solution.py:315
  26.7 2.9 %stage.7.refs_4_ = bf16[3,1024,1024]{2,1,0:T(8,128)(2,1)S(1)} custom-call(bf16[1,1024,16384]{2,1,0:T(8,128)(2,1)} %weight_ref.11, bf16[1,80,128]{2,1,0:T(8,128)(2,1)S(1)} %get-tuple-element.27.after_ref), custom_call_target="tpu_custom_call" | custom-call | flops 6291456 | bytes 6291456 | tf_op jit(solution)/shard_map/stage/pallas_call | solution.py:284
  29.6 2.5 %project_away.1 = (bf16[8,1024]{1,0:T(8,128)(2,1)S(1)}, bf16[4,8,2048]{2,1,0:T(8,128)(2,1)S(1)}) custom-call(bf16[1,80,128]{2,1,0:T(8,128)(2,1)S(1)} %get-tuple-element.26.kept_ref, bf16[1,80,128]{2,1,0:T(8,128)(2,1)S(1)} %collective-permute-done.6.got_ref, bf16[2,1024,1024]{2,1,0:T(8,128)(2,1)S(1)} %get-tuple-element.28.refs_0_, ...), custom_call_target="tpu_custom_call" | custom-call | flops 16777216 | bytes 16777216 | tf_op jit(solution)/shard_map/project_away/pallas_call | solution.py:284
  32.1 1.0 %collective-permute-start.7 = (bf16[4,8,2048]{2,1,0:T(8,128)(2,1)S(1)}, bf16[4,8,2048]{2,1,0:T(8,128)(2,1)S(1)}, u32[]{:S(2)}, u32[]{:S(2)}) collective-permute-start(bf16[4,8,2048]{2,1,0:T(8,128)(2,1)S(1)} %get-tuple-element.30), channel_id=1, source_target_pairs={{0,1},{1,0},{2,3},{3,2},{4,5},{5,4},{6,7},{7,6},{8,9},{9,8},{10,11... | collective-permute-start | bytes 393224 | tf_op jit(solution)/shard_map/ppermute | solution.py:315
  33.1 3.9 %project_own.1.kept_ref = f32[4,8,2048]{2,1,0:T(8,128)S(1)} custom-call(bf16[8,1024]{1,0:T(8,128)(2,1)S(1)} %get-tuple-element.29.flat_ref, bf16[1,1024,16384]{2,1,0:T(8,128)(2,1)} %weight_ref.11, bf16[2,1024,1024]{2,1,0:T(8,128)(2,1)S(1)} %get-tuple-element.28.refs_0_, bf16[2,1024,1024]{2,1,0:T(8,128)(2,1)S(1)} %stage.4.after_ref.refs_1_, ...), custom_call_target="tpu_custom_call" | custom-call | flops 16777216 | bytes 16777216 | tf_op jit(solution)/shard_map/project_own/pallas_call | solution.py:284
  37.2 1.8 %collective-permute-start.9 = (bf16[2,8,2048]{2,1,0:T(8,128)(2,1)S(1)}, bf16[2,8,2048]{2,1,0:T(8,128)(2,1)S(1)}, u32[]{:S(2)}, u32[]{:S(2)}) collective-permute-start(bf16[2,8,2048]{2,1,0:T(8,128)(2,1)S(1)} %get-tuple-element.31.near_ref), channel_id=1, source_target_pairs={{0,4},{1,5},{2,6},{3,7},{4,0},{5,1},{6,2},{7,3},{8,12},{9,13},{10,... | collective-permute-start | bytes 196616 | tf_op jit(solution)/shard_map/ppermute | solution.py:315
  39.0 1.4 %collective-permute-start.10 = (bf16[2,8,2048]{2,1,0:T(8,128)(2,1)S(1)}, bf16[2,8,2048]{2,1,0:T(8,128)(2,1)S(1)}, u32[]{:S(2)}, u32[]{:S(2)}) collective-permute-start(bf16[2,8,2048]{2,1,0:T(8,128)(2,1)S(1)} %get-tuple-element.32), channel_id=1, source_target_pairs={{0,6},{1,7},{2,4},{3,5},{4,2},{5,3},{6,0},{7,1},{8,14},{9,15},{10,... | collective-permute-start | bytes 196616 | tf_op jit(solution)/shard_map/ppermute | solution.py:315
  40.7 2.4 %collective-permute-done.9.two_ref = bf16[2,8,2048]{2,1,0:T(8,128)(2,1)S(1)} collective-permute-done((bf16[2,8,2048]{2,1,0:T(8,128)(2,1)S(1)}, bf16[2,8,2048]{2,1,0:T(8,128)(2,1)S(1)}, u32[]{:S(2)}, u32[]{:S(2)}) %collective-permute-start.9) | collective-permute-done | bytes 65568 | tf_op jit(solution)/shard_map/ppermute | solution.py:315
  43.1 2.1 %collective-permute-done.10.three_ref = bf16[2,8,2048]{2,1,0:T(8,128)(2,1)S(1)} collective-permute-done((bf16[2,8,2048]{2,1,0:T(8,128)(2,1)S(1)}, bf16[2,8,2048]{2,1,0:T(8,128)(2,1)S(1)}, u32[]{:S(2)}, u32[]{:S(2)}) %collective-permute-start.10) | collective-permute-done | bytes 65568 | tf_op jit(solution)/shard_map/ppermute | solution.py:315
  45.6 2.2 %collective-permute-start.13 = (bf16[2,8,2048]{2,1,0:T(8,128)(2,1)S(1)}, bf16[2,8,2048]{2,1,0:T(8,128)(2,1)S(1)}, u32[]{:S(2)}, u32[]{:S(2)}) collective-permute-start(bf16[2,8,2048]{2,1,0:T(8,128)(2,1)S(1)} %owner.1), channel_id=1, source_target_pairs={{0,10},{1,11},{2,8},{3,9},{4,14},{5,15},{6,12},{7,13},{8,2},{9,3},... | collective-permute-start | bytes 196616 | tf_op jit(solution)/shard_map/ppermute | solution.py:315
  47.8 1.1 %collective-permute-start.11 = (bf16[2,8,2048]{2,1,0:T(8,128)(2,1)S(1)}, bf16[2,8,2048]{2,1,0:T(8,128)(2,1)S(1)}, u32[]{:S(2)}, u32[]{:S(2)}) collective-permute-start(bf16[2,8,2048]{2,1,0:T(8,128)(2,1)S(1)} %owner.1), channel_id=1, source_target_pairs={{0,8},{1,9},{2,10},{3,11},{4,12},{5,13},{6,14},{7,15},{8,0},{9,1},... | collective-permute-start | bytes 196616 | tf_op jit(solution)/shard_map/ppermute | solution.py:315
  48.9 1.7 %collective-permute-done.14.refs_3_ = bf16[2,8,2048]{2,1,0:T(8,128)(2,1)S(1)} collective-permute-done((bf16[2,8,2048]{2,1,0:T(8,128)(2,1)S(1)}, bf16[2,8,2048]{2,1,0:T(8,128)(2,1)S(1)}, u32[]{:S(2)}, u32[]{:S(2)}) %collective-permute-start.14) | collective-permute-done | bytes 65568 | tf_op jit(solution)/shard_map/ppermute | solution.py:315
  51.8 0.7 %placed.1 = bf16[1,8,16384]{2,1,0:T(8,128)(2,1)} custom-call(bf16[2,8,2048]{2,1,0:T(8,128)(2,1)S(1)} %collective-permute-done.11.refs_0_, bf16[2,8,2048]{2,1,0:T(8,128)(2,1)S(1)} %collective-permute-done.12.refs_1_, bf16[2,8,2048]{2,1,0:T(8,128)(2,1)S(1)} %collective-permute-done.13.refs_2_, bf16[2,8,2048]{2,1,0:T(8,128)(2,1)S(1)} %collective-permute-done.14.refs_3_), custom_call_target="tpu_custom_call" | custom-call | flops 1048576 | bytes 1048576 | tf_op jit(solution)/shard_map/placed/pallas_call | solution.py:284
  (22 shorter events, 2.6 us)
Async XLA Ops:
  0.0 5.9 %collective-permute-start = (bf16[1,8,8,128]{3,2,1,0:T(8,128)(2,1)}, bf16[1,8,8,128]{3,2,1,0:T(8,128)(2,1)S(1)}, u32[]{:S(2)}, u32[]{:S(2)}) collective-permute-start(bf16[1,8,8,128]{3,2,1,0:T(8,128)(2,1)} %queries_ref.1), channel_id=1, source_target_pairs={{0,1},{1,0},{2,3},{3,2},{4,5},{5,4},{6,7},{7,6},{8,9},{9,8},{10,11... | collective-permute-start | bytes 49160 | tf_op jit(solution)/shard_map/ppermute | solution.py:315
  5.9 6.7 %collective-permute-start.3 = (bf16[2,8,8,128]{3,2,1,0:T(8,128)(2,1)S(1)}, bf16[2,8,8,128]{3,2,1,0:T(8,128)(2,1)S(1)}, u32[]{:S(2)}, u32[]{:S(2)}) collective-permute-start(bf16[2,8,8,128]{3,2,1,0:T(8,128)(2,1)S(1)} %append.1.after_ref.refs_0_), channel_id=1, source_target_pairs={{0,6},{1,7},{2,4},{3,5},{4,2},{5,3},{6,0},{7,1},{8,14},{9,15},{10,... | collective-permute-start | bytes 98312 | tf_op jit(solution)/shard_map/ppermute | solution.py:315
  9.6 4.8 %collective-permute-start.2 = (bf16[2,8,8,128]{3,2,1,0:T(8,128)(2,1)S(1)}, bf16[2,8,8,128]{3,2,1,0:T(8,128)(2,1)S(1)}, u32[]{:S(2)}, u32[]{:S(2)}) collective-permute-start(bf16[2,8,8,128]{3,2,1,0:T(8,128)(2,1)S(1)} %append.1.after_ref.refs_0_), channel_id=1, source_target_pairs={{0,4},{1,5},{2,6},{3,7},{4,0},{5,1},{6,2},{7,3},{8,12},{9,13},{10,... | collective-permute-start | bytes 98312 | tf_op jit(solution)/shard_map/ppermute | solution.py:315
  9.6 4.8 %collective-permute-start.1 = (bf16[2,8,8,128]{3,2,1,0:T(8,128)(2,1)S(1)}, bf16[2,8,8,128]{3,2,1,0:T(8,128)(2,1)S(1)}, u32[]{:S(2)}, u32[]{:S(2)}) collective-permute-start(bf16[2,8,8,128]{3,2,1,0:T(8,128)(2,1)S(1)} %append.1.after_ref.refs_0_), channel_id=1, source_target_pairs={{0,2},{1,3},{2,0},{3,1},{4,6},{5,7},{6,4},{7,5},{8,10},{9,11},{10,... | collective-permute-start | bytes 98312 | tf_op jit(solution)/shard_map/ppermute | solution.py:315
  15.5 4.5 %collective-permute-start.4 = (bf16[4,80,128]{2,1,0:T(8,128)(2,1)S(1)}, bf16[4,80,128]{2,1,0:T(8,128)(2,1)S(1)}, u32[]{:S(2)}, u32[]{:S(2)}) collective-permute-start(bf16[4,80,128]{2,1,0:T(8,128)(2,1)S(1)} %get-tuple-element.22.after_ref), channel_id=1, source_target_pairs={{0,1},{1,0},{2,3},{3,2},{4,5},{5,4},{6,7},{7,6},{8,9},{9,8},{10,11... | collective-permute-start | bytes 245768 | tf_op jit(solution)/shard_map/ppermute | solution.py:315
  20.2 4.1 %collective-permute-start.5 = (bf16[2,80,128]{2,1,0:T(8,128)(2,1)S(1)}, bf16[2,80,128]{2,1,0:T(8,128)(2,1)S(1)}, u32[]{:S(2)}, u32[]{:S(2)}) collective-permute-start(bf16[2,80,128]{2,1,0:T(8,128)(2,1)S(1)} %get-tuple-element.24.after_ref), channel_id=1, source_target_pairs={{0,2},{1,3},{2,0},{3,1},{4,6},{5,7},{6,4},{7,5},{8,10},{9,11},{10,... | collective-permute-start | bytes 122888 | tf_op jit(solution)/shard_map/ppermute | solution.py:315
  24.4 5.2 %collective-permute-start.6 = (bf16[1,80,128]{2,1,0:T(8,128)(2,1)S(1)}, bf16[1,80,128]{2,1,0:T(8,128)(2,1)S(1)}, u32[]{:S(2)}, u32[]{:S(2)}) collective-permute-start(bf16[1,80,128]{2,1,0:T(8,128)(2,1)S(1)} %get-tuple-element.27.after_ref), channel_id=1, source_target_pairs={{0,4},{1,5},{2,6},{3,7},{4,0},{5,1},{6,2},{7,3},{8,12},{9,13},{10,... | collective-permute-start | bytes 61448 | tf_op jit(solution)/shard_map/ppermute | solution.py:315
  32.1 5.0 %collective-permute-start.7 = (bf16[4,8,2048]{2,1,0:T(8,128)(2,1)S(1)}, bf16[4,8,2048]{2,1,0:T(8,128)(2,1)S(1)}, u32[]{:S(2)}, u32[]{:S(2)}) collective-permute-start(bf16[4,8,2048]{2,1,0:T(8,128)(2,1)S(1)} %get-tuple-element.30), channel_id=1, source_target_pairs={{0,1},{1,0},{2,3},{3,2},{4,5},{5,4},{6,7},{7,6},{8,9},{9,8},{10,11... | collective-permute-start | bytes 393224 | tf_op jit(solution)/shard_map/ppermute | solution.py:315
  33.1 4.1 %copy-start = (bf16[1,8,2048]{2,1,0:T(8,128)(2,1)S(1)}, bf16[1,8,2048]{2,1,0:T(8,128)(2,1)}, u32[]{:S(2)}) copy-start(bf16[1,8,2048]{2,1,0:T(8,128)(2,1)} %residual_ref.1) | copy-start | bytes 98308
  37.2 5.9 %collective-permute-start.9 = (bf16[2,8,2048]{2,1,0:T(8,128)(2,1)S(1)}, bf16[2,8,2048]{2,1,0:T(8,128)(2,1)S(1)}, u32[]{:S(2)}, u32[]{:S(2)}) collective-permute-start(bf16[2,8,2048]{2,1,0:T(8,128)(2,1)S(1)} %get-tuple-element.31.near_ref), channel_id=1, source_target_pairs={{0,4},{1,5},{2,6},{3,7},{4,0},{5,1},{6,2},{7,3},{8,12},{9,13},{10,... | collective-permute-start | bytes 196616 | tf_op jit(solution)/shard_map/ppermute | solution.py:315
  39.0 6.2 %collective-permute-start.10 = (bf16[2,8,2048]{2,1,0:T(8,128)(2,1)S(1)}, bf16[2,8,2048]{2,1,0:T(8,128)(2,1)S(1)}, u32[]{:S(2)}, u32[]{:S(2)}) collective-permute-start(bf16[2,8,2048]{2,1,0:T(8,128)(2,1)S(1)} %get-tuple-element.32), channel_id=1, source_target_pairs={{0,6},{1,7},{2,4},{3,5},{4,2},{5,3},{6,0},{7,1},{8,14},{9,15},{10,... | collective-permute-start | bytes 196616 | tf_op jit(solution)/shard_map/ppermute | solution.py:315
  40.4 5.0 %collective-permute-start.8 = (bf16[2,8,2048]{2,1,0:T(8,128)(2,1)S(1)}, bf16[2,8,2048]{2,1,0:T(8,128)(2,1)S(1)}, u32[]{:S(2)}, u32[]{:S(2)}) collective-permute-start(bf16[2,8,2048]{2,1,0:T(8,128)(2,1)S(1)} %get-tuple-element.32), channel_id=1, source_target_pairs={{0,2},{1,3},{2,0},{3,1},{4,6},{5,7},{6,4},{7,5},{8,10},{9,11},{10,... | collective-permute-start | bytes 196616 | tf_op jit(solution)/shard_map/ppermute | solution.py:315
  45.5 5.0 %collective-permute-start.14 = (bf16[2,8,2048]{2,1,0:T(8,128)(2,1)S(1)}, bf16[2,8,2048]{2,1,0:T(8,128)(2,1)S(1)}, u32[]{:S(2)}, u32[]{:S(2)}) collective-permute-start(bf16[2,8,2048]{2,1,0:T(8,128)(2,1)S(1)} %owner.1), channel_id=1, source_target_pairs={{0,11},{1,10},{2,9},{3,8},{4,15},{5,14},{6,13},{7,12},{8,3},{9,2},... | collective-permute-start | bytes 196616 | tf_op jit(solution)/shard_map/ppermute | solution.py:315
  45.6 5.6 %collective-permute-start.13 = (bf16[2,8,2048]{2,1,0:T(8,128)(2,1)S(1)}, bf16[2,8,2048]{2,1,0:T(8,128)(2,1)S(1)}, u32[]{:S(2)}, u32[]{:S(2)}) collective-permute-start(bf16[2,8,2048]{2,1,0:T(8,128)(2,1)S(1)} %owner.1), channel_id=1, source_target_pairs={{0,10},{1,11},{2,8},{3,9},{4,14},{5,15},{6,12},{7,13},{8,2},{9,3},... | collective-permute-start | bytes 196616 | tf_op jit(solution)/shard_map/ppermute | solution.py:315
  47.8 4.0 %collective-permute-start.12 = (bf16[2,8,2048]{2,1,0:T(8,128)(2,1)S(1)}, bf16[2,8,2048]{2,1,0:T(8,128)(2,1)S(1)}, u32[]{:S(2)}, u32[]{:S(2)}) collective-permute-start(bf16[2,8,2048]{2,1,0:T(8,128)(2,1)S(1)} %owner.1), channel_id=1, source_target_pairs={{0,9},{1,8},{2,11},{3,10},{4,13},{5,12},{6,15},{7,14},{8,1},{9,0},... | collective-permute-start | bytes 196616 | tf_op jit(solution)/shard_map/ppermute | solution.py:315
  47.8 4.0 %collective-permute-start.11 = (bf16[2,8,2048]{2,1,0:T(8,128)(2,1)S(1)}, bf16[2,8,2048]{2,1,0:T(8,128)(2,1)S(1)}, u32[]{:S(2)}, u32[]{:S(2)}) collective-permute-start(bf16[2,8,2048]{2,1,0:T(8,128)(2,1)S(1)} %owner.1), channel_id=1, source_target_pairs={{0,8},{1,9},{2,10},{3,11},{4,12},{5,13},{6,14},{7,15},{8,0},{9,1},... | collective-permute-start | bytes 196616 | tf_op jit(solution)/shard_map/ppermute | solution.py:315

commit v2 on v0

--- a/solution.py
+++ b/solution.py
@@ -135,7 +135,7 @@
 
 def place(k, tp):
     quarter = tp // 4
-    at = k % quarter * 4 + k // quarter
+    at = k % quarter * 4 + (4 - k // quarter) % 4
     return at // (tp // 2), at % (tp // 2)
 
 
@@ -218,8 +218,12 @@
         project_columns(flat, held[array].at[index], out_ref, i // 2, i % 2 * columns)
 
 
-def project_away_kernel(rows, heads, places, *refs):
-    sources, held, (flat_ref, out_ref) = refs[:4], refs[4:-2], refs[-2:]
+def project_away_kernel(rows, heads, places, units, *refs):
+    sources, weight_ref, held = refs[:4], refs[4], refs[5:-4]
+    flat_ref, out_ref, later_ref, sems = refs[-4:]
+    copies = weight_copies(units, weight_ref, later_ref, sems)
+    for copy in copies:
+        copy.start()
     mixed, _, total = merged([source[0] for source in sources])
     attended = mixed / to_column(total, mixed.shape[0])
     flat = jnp.concatenate(
@@ -227,6 +231,8 @@
     ).astype(BF16)
     flat_ref[...] = flat
     project_units(flat, held, places, out_ref)
+    for copy in copies:
+        copy.wait()
 
 
 def project_own_kernel(places, units, flat_ref, weight_ref, *refs):
@@ -249,18 +255,19 @@
         keep_ref[i] = kept_ref[2 * i] + got_ref[2 * i].astype(F32)
 
 
-def pair_kernel(kept_ref, got_ref, residual_ref, even_ref, odd_ref):
+def pair_kernel(kept_ref, got_ref, residual_ref, far_ref, even_ref, odd_ref):
     for i in range(4):
         x = kept_ref[i] + got_ref[i].astype(F32)
         if i == 0:
             x = x + residual_ref[0].astype(F32)
         if i & 1:
             odd_ref[i >> 1] = x.astype(BF16)
+            far_ref[i >> 1] = x.astype(BF16)
         else:
             even_ref[i >> 1] = x.astype(BF16)
 
 
-def owner_kernel(near_ref, one_ref, two_ref, three_ref, out_ref):
+def owner_kernel(three_ref, two_ref, one_ref, near_ref, out_ref):
     for i in range(2):
         for b in range(0, out_ref.shape[2], QB):
             at = slice(b, b + QB)
@@ -375,7 +382,7 @@
             got = exchanged(have, 2 << b)
     all_queries = [have, *(exchanged(have, k) for k in reversed(groups))]
     all_queries[1:] = all_queries[:0:-1]
-    after = stage(have, 5)
+    after = stage(have, 2)
     packed_block = (heads * rows + STAT_ROWS, dim)
     kept, send = call(
         attention_kernel,
@@ -397,23 +404,25 @@
         merge_kernel, "merge", [struct((1, *packed_block), BF16)] * 4, (after, kept, got)
     )
     last = pending[3]
-    pending = [pending[0], *(exchanged(block, k) for block, k in zip(pending[1:], groups))]
-    stage(last, 3)
-
-    where = {
-        unit: (array, i) for array, (units, _) in enumerate(staged) for i, unit in enumerate(units)
-    }
-    places = [where[unit] for unit in order if unit in where]
+    pending = [pending[0], *(exchanged(block, k) for block, k in zip(pending[1:], groups[::-1]))]
+    stage(last, 4)
+
+    held = [array for _, array in staged]
+    places = [(a, i) for a, (units, _) in enumerate(staged) for i in range(len(units))]
+    units = next_units(2)
+    flat, away, later = call(
+        functools.partial(project_away_kernel, rows, heads, places[:tp], units),
+        "project_away",
+        [struct((rows, depth), BF16), struct((half, rows, width), BF16), held_shape(units)],
+        (*pending, weight, *held),
+        in_specs=[VMEM_SPEC] * 4 + [ANY_SPEC] + [VMEM_SPEC] * len(held),
+        scratch=[pltpu.SemaphoreType.DMA((len(units),))],
+        cost=16 * MIB,
+    )
+    got = exchanged(away, 1)
+    places += [(len(held), i) for i in range(len(units))]
+    held.append(later)
     late = order[len(places) :]
-    held = [array for _, array in staged]
-    flat, away = call(
-        functools.partial(project_away_kernel, rows, heads, places[:tp]),
-        "project_away",
-        [struct((rows, depth), BF16), struct((half, rows, width), BF16)],
-        (*pending, *held),
-        cost=16 * MIB,
-    )
-    got = exchanged(away, 1)
     kept = call(
         functools.partial(project_own_kernel, places[tp:], late),
         "project_own",
@@ -436,14 +445,14 @@
             (kept, got),
         )
         got = exchanged(send, 1 << b)
-    even, odd = call(
-        pair_kernel, "pair_sum", [struct((2, rows, width), BF16)] * 2, (kept, got, residual)
-    )
-    three = exchanged(odd, groups[2])
+    far, even, odd = call(
+        pair_kernel, "pair_sum", [struct((2, rows, width), BF16)] * 3, (kept, got, residual)
+    )
+    three = exchanged(far, groups[2])
     two = exchanged(even, groups[1])
     one = exchanged(odd, groups[0])
     own = call(
-        owner_kernel, "owner", struct((2, rows, width), BF16), (even, one, two, three)
+        owner_kernel, "owner", struct((2, rows, width), BF16), (three, two, one, even)
     )
     high = 1 << (bits - 1)
     parts = [(k, exchanged(own, k, 1)) for k in range(high)]

time: 51.9 us -> 51.4 us (level)
  starting transfers between devices: 21 us -> 21.9 us
  Pallas kernels: 22 us -> 21.3 us
  waiting for transfers between devices: 8.59 us -> 7.98 us
    ppermute x16, starting transfers between devices: 21 us -> 21.9 us  [exchanged(): return lax.ppermute(array, ('section', 'tp'), pairs)]
    pallas_call x12, Pallas kernels: 22 us -> 21.3 us  [call(): pl.pallas_call(kernel, out_shape=outs, in_specs=in_specs or [VMEM_SPEC] *...]
    ppermute x16, waiting for transfers between devices: 8.59 us -> 7.98 us  [exchanged(): return lax.ppermute(array, ('section', 'tp'), pairs)]
  transfers between devices with their start and end apart: 16 -> 16, of which waited for: 7 -> 6; matrix products, arithmetic and copies ran while one was open for 0% -> 0% of each run, Pallas kernels for 34% -> 32%
where the time goes in v2:
time: 51.4 us; the launch traced here: 51.3 us
  starting transfers between devices  21.9 us (43%)
  Pallas kernels  21.3 us (41%)
  waiting for transfers between devices  7.98 us (16%)
    ppermute x16, starting transfers between devices, exchanged(): return lax.ppermute(array, ('section', 'tp'), pairs)  21.9 us
    pallas_call x12, Pallas kernels, call(): pl.pallas_call(kernel, out_shape=outs, in_specs=in_specs or [VMEM_SPEC] *...  21.3 us
    ppermute x16, waiting for transfers between devices, exchanged(): return lax.ppermute(array, ('section', 'tp'), pairs)  7.98 us
  transfers between devices with their start and end apart: 16, of which 6 were waited for; matrix products, arithmetic and copies ran while one was open for 0% of the time, Pallas kernels for 32%

profile of v2, /device:TPU:0, one launch (start us, length us, event | category | flops | bytes accessed | tf_op | source)
XLA Modules:
  0.0 51.3 jit_solution(3964182674120796621)
XLA Ops:
  0.0 3.0 %collective-permute-start = (bf16[1,8,8,128]{3,2,1,0:T(8,128)(2,1)}, bf16[1,8,8,128]{3,2,1,0:T(8,128)(2,1)S(1)}, u32[]{:S(2)}, u32[]{:S(2)}) collective-permute-start(bf16[1,8,8,128]{3,2,1,0:T(8,128)(2,1)} %queries_ref.1), channel_id=1, source_target_pairs={{0,1},{1,0},{2,3},{3,2},{4,5},{5,4},{6,7},{7,6},{8,9},{9,8},{10,11... | collective-permute-start | bytes 49160 | tf_op jit(solution)/shard_map/ppermute | solution.py:321
  3.0 2.9 %stage_cache.1 = (bf16[8,2,4,128,128]{4,3,2,1,0:T(8,128)(2,1)S(1)}, s32[8,128]{1,0:T(8,128)S(1)}, bf16[1,8,8,128]{3,2,1,0:T(8,128)(2,1)S(1)}, bf16[2,1024,1024]{2,1,0:T(8,128)(2,1)S(1)}) custom-call(s32[1,8]{1,0:T(1,128)} %lengths_ref.1, bf16[1,8,2,4,128]{4,3,2,1,0:T(4,128)(2,1)} %new_ref.1, bf16[1,8,2,4,128,128]{5,4,3,2,1,0:T(8,128)(2,1)} %kv_ref.1, ...), custom_call_target="tpu_custom_call" | custom-call | flops 8388608 | bytes 8388608 | tf_op jit(solution)/shard_map/stage_cache/pallas_call | solution.py:290
  5.9 3.7 %collective-permute-start.3 = (bf16[2,8,8,128]{3,2,1,0:T(8,128)(2,1)S(1)}, bf16[2,8,8,128]{3,2,1,0:T(8,128)(2,1)S(1)}, u32[]{:S(2)}, u32[]{:S(2)}) collective-permute-start(bf16[2,8,8,128]{3,2,1,0:T(8,128)(2,1)S(1)} %append.1.after_ref.refs_0_), channel_id=1, source_target_pairs={{0,6},{1,7},{2,4},{3,5},{4,2},{5,3},{6,0},{7,1},{8,14},{9,15},{10,... | collective-permute-start | bytes 98312 | tf_op jit(solution)/shard_map/ppermute | solution.py:321
  9.6 0.8 %collective-permute-start.1 = (bf16[2,8,8,128]{3,2,1,0:T(8,128)(2,1)S(1)}, bf16[2,8,8,128]{3,2,1,0:T(8,128)(2,1)S(1)}, u32[]{:S(2)}, u32[]{:S(2)}) collective-permute-start(bf16[2,8,8,128]{3,2,1,0:T(8,128)(2,1)S(1)} %append.1.after_ref.refs_0_), channel_id=1, source_target_pairs={{0,2},{1,3},{2,0},{3,1},{4,6},{5,7},{6,4},{7,5},{8,10},{9,11},{10,... | collective-permute-start | bytes 98312 | tf_op jit(solution)/shard_map/ppermute | solution.py:321
  10.4 2.2 %stage.3.after_ref.refs_6_.refs_1_ = bf16[2,1024,1024]{2,1,0:T(8,128)(2,1)S(1)} custom-call(bf16[1,1024,16384]{2,1,0:T(8,128)(2,1)} %weight_ref.9, bf16[2,8,8,128]{3,2,1,0:T(8,128)(2,1)S(1)} %append.1.after_ref.refs_0_), custom_call_target="tpu_custom_call" | custom-call | flops 4194304 | bytes 4194304 | tf_op jit(solution)/shard_map/stage/pallas_call | solution.py:290
  12.7 1.8 %collective-permute-done.2.refs_2_ = bf16[2,8,8,128]{3,2,1,0:T(8,128)(2,1)S(1)} collective-permute-done((bf16[2,8,8,128]{3,2,1,0:T(8,128)(2,1)S(1)}, bf16[2,8,8,128]{3,2,1,0:T(8,128)(2,1)S(1)}, u32[]{:S(2)}, u32[]{:S(2)}) %collective-permute-start.2) | collective-permute-done | bytes 32800 | tf_op jit(solution)/shard_map/ppermute | solution.py:321
  14.4 1.1 %attention.1 = (bf16[4,80,128]{2,1,0:T(8,128)(2,1)S(1)}, bf16[4,80,128]{2,1,0:T(8,128)(2,1)S(1)}) custom-call(bf16[8,2,4,128,128]{4,3,2,1,0:T(8,128)(2,1)S(1)} %get-tuple-element.21.stored_ref, s32[8,128]{1,0:T(8,128)S(1)} %get-tuple-element.22.after_ref.limit_ref, bf16[2,1024,1024]{2,1,0:T(8,128)(2,1)S(1)} %stage.3.after_ref.refs_6_.refs_1_, ...), custom_call_target="tpu_custom_call" | custom-call | flops 8388608 | bytes 8388608 | tf_op jit(solution)/shard_map/attention/pallas_call | solution.py:290
  15.5 1.0 %collective-permute-start.4 = (bf16[4,80,128]{2,1,0:T(8,128)(2,1)S(1)}, bf16[4,80,128]{2,1,0:T(8,128)(2,1)S(1)}, u32[]{:S(2)}, u32[]{:S(2)}) collective-permute-start(bf16[4,80,128]{2,1,0:T(8,128)(2,1)S(1)} %get-tuple-element.24.after_ref), channel_id=1, source_target_pairs={{0,1},{1,0},{2,3},{3,2},{4,5},{5,4},{6,7},{7,6},{8,9},{9,8},{10,11... | collective-permute-start | bytes 245768 | tf_op jit(solution)/shard_map/ppermute | solution.py:321
  16.5 3.5 %stage.4.after_ref.refs_7_.refs_2_ = bf16[4,1024,1024]{2,1,0:T(8,128)(2,1)S(1)} custom-call(bf16[1,1024,16384]{2,1,0:T(8,128)(2,1)} %weight_ref.9, bf16[4,80,128]{2,1,0:T(8,128)(2,1)S(1)} %get-tuple-element.24.after_ref), custom_call_target="tpu_custom_call" | custom-call | flops 8388608 | bytes 8388608 | tf_op jit(solution)/shard_map/stage/pallas_call | solution.py:290
  20.2 1.9 %collective-permute-start.5 = (bf16[1,80,128]{2,1,0:T(8,128)(2,1)S(1)}, bf16[1,80,128]{2,1,0:T(8,128)(2,1)S(1)}, u32[]{:S(2)}, u32[]{:S(2)}) collective-permute-start(bf16[1,80,128]{2,1,0:T(8,128)(2,1)S(1)} %get-tuple-element.27), channel_id=1, source_target_pairs={{0,6},{1,7},{2,4},{3,5},{4,2},{5,3},{6,0},{7,1},{8,14},{9,15},{10,... | collective-permute-start | bytes 61448 | tf_op jit(solution)/shard_map/ppermute | solution.py:321
  22.4 2.3 %collective-permute-start.7 = (bf16[1,80,128]{2,1,0:T(8,128)(2,1)S(1)}, bf16[1,80,128]{2,1,0:T(8,128)(2,1)S(1)}, u32[]{:S(2)}, u32[]{:S(2)}) collective-permute-start(bf16[1,80,128]{2,1,0:T(8,128)(2,1)S(1)} %get-tuple-element.29.after_ref), channel_id=1, source_target_pairs={{0,2},{1,3},{2,0},{3,1},{4,6},{5,7},{6,4},{7,5},{8,10},{9,11},{10,... | collective-permute-start | bytes 61448 | tf_op jit(solution)/shard_map/ppermute | solution.py:321
  24.7 3.5 %stage.5.refs_8_.refs_3_ = bf16[4,1024,1024]{2,1,0:T(8,128)(2,1)S(1)} custom-call(bf16[1,1024,16384]{2,1,0:T(8,128)(2,1)} %weight_ref.9, bf16[1,80,128]{2,1,0:T(8,128)(2,1)S(1)} %get-tuple-element.29.after_ref), custom_call_target="tpu_custom_call" | custom-call | flops 8388608 | bytes 8388608 | tf_op jit(solution)/shard_map/stage/pallas_call | solution.py:290
  28.2 2.9 %project_away.1 = (bf16[8,1024]{1,0:T(8,128)(2,1)S(1)}, bf16[4,8,2048]{2,1,0:T(8,128)(2,1)S(1)}, bf16[2,1024,1024]{2,1,0:T(8,128)(2,1)S(1)}) custom-call(bf16[1,80,128]{2,1,0:T(8,128)(2,1)S(1)} %get-tuple-element.26.refs_0_, bf16[1,80,128]{2,1,0:T(8,128)(2,1)S(1)} %collective-permute-done.5.refs_1_, bf16[1,80,128]{2,1,0:T(8,128)(2,1)S(1)} %collective-permute-done.6.refs_2_, ...), custom_call_target="tpu_custom_call" | custom-call | flops 16777216 | bytes 16777216 | tf_op jit(solution)/shard_map/project_away/pallas_call | solution.py:290
  31.2 1.2 %collective-permute-start.8 = (bf16[4,8,2048]{2,1,0:T(8,128)(2,1)S(1)}, bf16[4,8,2048]{2,1,0:T(8,128)(2,1)S(1)}, u32[]{:S(2)}, u32[]{:S(2)}) collective-permute-start(bf16[4,8,2048]{2,1,0:T(8,128)(2,1)S(1)} %get-tuple-element.33), channel_id=1, source_target_pairs={{0,1},{1,0},{2,3},{3,2},{4,5},{5,4},{6,7},{7,6},{8,9},{9,8},{10,11... | collective-permute-start | bytes 393224 | tf_op jit(solution)/shard_map/ppermute | solution.py:321
  32.3 3.9 %project_own.1.kept_ref = f32[4,8,2048]{2,1,0:T(8,128)S(1)} custom-call(bf16[8,1024]{1,0:T(8,128)(2,1)S(1)} %get-tuple-element.31.flat_ref, bf16[1,1024,16384]{2,1,0:T(8,128)(2,1)} %weight_ref.9, bf16[2,1024,1024]{2,1,0:T(8,128)(2,1)S(1)} %get-tuple-element.30.refs_5_.refs_0_, bf16[2,1024,1024]{2,1,0:T(8,128)(2,1)S(1)} %stage.3.after_ref.refs_6_.refs_1_, ...), custom_call_target="tpu_custom_call" | custom-call | flops 16777216 | bytes 16777216 | tf_op jit(solution)/shard_map/project_own/pallas_call | solution.py:290
  36.3 1.9 %collective-permute-start.9 = (bf16[2,8,2048]{2,1,0:T(8,128)(2,1)S(1)}, bf16[2,8,2048]{2,1,0:T(8,128)(2,1)S(1)}, u32[]{:S(2)}, u32[]{:S(2)}) collective-permute-start(bf16[2,8,2048]{2,1,0:T(8,128)(2,1)S(1)} %get-tuple-element.34), channel_id=1, source_target_pairs={{0,6},{1,7},{2,4},{3,5},{4,2},{5,3},{6,0},{7,1},{8,14},{9,15},{10,... | collective-permute-start | bytes 196616 | tf_op jit(solution)/shard_map/ppermute | solution.py:321
  38.3 2.5 %collective-permute-start.10 = (bf16[2,8,2048]{2,1,0:T(8,128)(2,1)S(1)}, bf16[2,8,2048]{2,1,0:T(8,128)(2,1)S(1)}, u32[]{:S(2)}, u32[]{:S(2)}) collective-permute-start(bf16[2,8,2048]{2,1,0:T(8,128)(2,1)S(1)} %get-tuple-element.35.near_ref), channel_id=1, source_target_pairs={{0,4},{1,5},{2,6},{3,7},{4,0},{5,1},{6,2},{7,3},{8,12},{9,13},{10,... | collective-permute-start | bytes 196616 | tf_op jit(solution)/shard_map/ppermute | solution.py:321
  40.8 1.7 %collective-permute-done.9.three_ref = bf16[2,8,2048]{2,1,0:T(8,128)(2,1)S(1)} collective-permute-done((bf16[2,8,2048]{2,1,0:T(8,128)(2,1)S(1)}, bf16[2,8,2048]{2,1,0:T(8,128)(2,1)S(1)}, u32[]{:S(2)}, u32[]{:S(2)}) %collective-permute-start.9) | collective-permute-done | bytes 65568 | tf_op jit(solution)/shard_map/ppermute | solution.py:321
  42.5 1.3 %collective-permute-done.11.one_ref = bf16[2,8,2048]{2,1,0:T(8,128)(2,1)S(1)} collective-permute-done((bf16[2,8,2048]{2,1,0:T(8,128)(2,1)S(1)}, bf16[2,8,2048]{2,1,0:T(8,128)(2,1)S(1)}, u32[]{:S(2)}, u32[]{:S(2)}) %collective-permute-start.11) | collective-permute-done | bytes 65568 | tf_op jit(solution)/shard_map/ppermute | solution.py:321
  44.1 2.2 %collective-permute-start.14 = (bf16[2,8,2048]{2,1,0:T(8,128)(2,1)S(1)}, bf16[2,8,2048]{2,1,0:T(8,128)(2,1)S(1)}, u32[]{:S(2)}, u32[]{:S(2)}) collective-permute-start(bf16[2,8,2048]{2,1,0:T(8,128)(2,1)S(1)} %owner.1), channel_id=1, source_target_pairs={{0,10},{1,11},{2,8},{3,9},{4,14},{5,15},{6,12},{7,13},{8,2},{9,3},... | collective-permute-start | bytes 196616 | tf_op jit(solution)/shard_map/ppermute | solution.py:321
  46.3 0.6 %collective-permute-start.13 = (bf16[2,8,2048]{2,1,0:T(8,128)(2,1)S(1)}, bf16[2,8,2048]{2,1,0:T(8,128)(2,1)S(1)}, u32[]{:S(2)}, u32[]{:S(2)}) collective-permute-start(bf16[2,8,2048]{2,1,0:T(8,128)(2,1)S(1)} %owner.1), channel_id=1, source_target_pairs={{0,9},{1,8},{2,11},{3,10},{4,13},{5,12},{6,15},{7,14},{8,1},{9,0},... | collective-permute-start | bytes 196616 | tf_op jit(solution)/shard_map/ppermute | solution.py:321
  47.4 1.6 %collective-permute-done.15.refs_3_ = bf16[2,8,2048]{2,1,0:T(8,128)(2,1)S(1)} collective-permute-done((bf16[2,8,2048]{2,1,0:T(8,128)(2,1)S(1)}, bf16[2,8,2048]{2,1,0:T(8,128)(2,1)S(1)}, u32[]{:S(2)}, u32[]{:S(2)}) %collective-permute-start.15) | collective-permute-done | bytes 65568 | tf_op jit(solution)/shard_map/ppermute | solution.py:321
  49.3 1.2 %collective-permute-done.13.refs_1_ = bf16[2,8,2048]{2,1,0:T(8,128)(2,1)S(1)} collective-permute-done((bf16[2,8,2048]{2,1,0:T(8,128)(2,1)S(1)}, bf16[2,8,2048]{2,1,0:T(8,128)(2,1)S(1)}, u32[]{:S(2)}, u32[]{:S(2)}) %collective-permute-start.13) | collective-permute-done | bytes 65568 | tf_op jit(solution)/shard_map/ppermute | solution.py:321
  50.5 0.7 %placed.1 = bf16[1,8,16384]{2,1,0:T(8,128)(2,1)} custom-call(bf16[2,8,2048]{2,1,0:T(8,128)(2,1)S(1)} %collective-permute-done.12.refs_0_, bf16[2,8,2048]{2,1,0:T(8,128)(2,1)S(1)} %collective-permute-done.13.refs_1_, bf16[2,8,2048]{2,1,0:T(8,128)(2,1)S(1)} %collective-permute-done.14.refs_2_, bf16[2,8,2048]{2,1,0:T(8,128)(2,1)S(1)} %collective-permute-done.15.refs_3_), custom_call_target="tpu_custom_call" | custom-call | flops 1048576 | bytes 1048576 | tf_op jit(solution)/shard_map/placed/pallas_call | solution.py:290
  (22 shorter events, 1.5 us)
Async XLA Ops:
  0.0 5.9 %collective-permute-start = (bf16[1,8,8,128]{3,2,1,0:T(8,128)(2,1)}, bf16[1,8,8,128]{3,2,1,0:T(8,128)(2,1)S(1)}, u32[]{:S(2)}, u32[]{:S(2)}) collective-permute-start(bf16[1,8,8,128]{3,2,1,0:T(8,128)(2,1)} %queries_ref.1), channel_id=1, source_target_pairs={{0,1},{1,0},{2,3},{3,2},{4,5},{5,4},{6,7},{7,6},{8,9},{9,8},{10,11... | collective-permute-start | bytes 49160 | tf_op jit(solution)/shard_map/ppermute | solution.py:321
  5.9 6.7 %collective-permute-start.3 = (bf16[2,8,8,128]{3,2,1,0:T(8,128)(2,1)S(1)}, bf16[2,8,8,128]{3,2,1,0:T(8,128)(2,1)S(1)}, u32[]{:S(2)}, u32[]{:S(2)}) collective-permute-start(bf16[2,8,8,128]{3,2,1,0:T(8,128)(2,1)S(1)} %append.1.after_ref.refs_0_), channel_id=1, source_target_pairs={{0,6},{1,7},{2,4},{3,5},{4,2},{5,3},{6,0},{7,1},{8,14},{9,15},{10,... | collective-permute-start | bytes 98312 | tf_op jit(solution)/shard_map/ppermute | solution.py:321
  9.6 4.8 %collective-permute-start.2 = (bf16[2,8,8,128]{3,2,1,0:T(8,128)(2,1)S(1)}, bf16[2,8,8,128]{3,2,1,0:T(8,128)(2,1)S(1)}, u32[]{:S(2)}, u32[]{:S(2)}) collective-permute-start(bf16[2,8,8,128]{3,2,1,0:T(8,128)(2,1)S(1)} %append.1.after_ref.refs_0_), channel_id=1, source_target_pairs={{0,4},{1,5},{2,6},{3,7},{4,0},{5,1},{6,2},{7,3},{8,12},{9,13},{10,... | collective-permute-start | bytes 98312 | tf_op jit(solution)/shard_map/ppermute | solution.py:321
  9.6 4.8 %collective-permute-start.1 = (bf16[2,8,8,128]{3,2,1,0:T(8,128)(2,1)S(1)}, bf16[2,8,8,128]{3,2,1,0:T(8,128)(2,1)S(1)}, u32[]{:S(2)}, u32[]{:S(2)}) collective-permute-start(bf16[2,8,8,128]{3,2,1,0:T(8,128)(2,1)S(1)} %append.1.after_ref.refs_0_), channel_id=1, source_target_pairs={{0,2},{1,3},{2,0},{3,1},{4,6},{5,7},{6,4},{7,5},{8,10},{9,11},{10,... | collective-permute-start | bytes 98312 | tf_op jit(solution)/shard_map/ppermute | solution.py:321
  15.5 4.5 %collective-permute-start.4 = (bf16[4,80,128]{2,1,0:T(8,128)(2,1)S(1)}, bf16[4,80,128]{2,1,0:T(8,128)(2,1)S(1)}, u32[]{:S(2)}, u32[]{:S(2)}) collective-permute-start(bf16[4,80,128]{2,1,0:T(8,128)(2,1)S(1)} %get-tuple-element.24.after_ref), channel_id=1, source_target_pairs={{0,1},{1,0},{2,3},{3,2},{4,5},{5,4},{6,7},{7,6},{8,9},{9,8},{10,11... | collective-permute-start | bytes 245768 | tf_op jit(solution)/shard_map/ppermute | solution.py:321
  20.2 8.0 %collective-permute-start.5 = (bf16[1,80,128]{2,1,0:T(8,128)(2,1)S(1)}, bf16[1,80,128]{2,1,0:T(8,128)(2,1)S(1)}, u32[]{:S(2)}, u32[]{:S(2)}) collective-permute-start(bf16[1,80,128]{2,1,0:T(8,128)(2,1)S(1)} %get-tuple-element.27), channel_id=1, source_target_pairs={{0,6},{1,7},{2,4},{3,5},{4,2},{5,3},{6,0},{7,1},{8,14},{9,15},{10,... | collective-permute-start | bytes 61448 | tf_op jit(solution)/shard_map/ppermute | solution.py:321
  22.2 6.1 %collective-permute-start.6 = (bf16[1,80,128]{2,1,0:T(8,128)(2,1)S(1)}, bf16[1,80,128]{2,1,0:T(8,128)(2,1)S(1)}, u32[]{:S(2)}, u32[]{:S(2)}) collective-permute-start(bf16[1,80,128]{2,1,0:T(8,128)(2,1)S(1)} %get-tuple-element.28), channel_id=1, source_target_pairs={{0,4},{1,5},{2,6},{3,7},{4,0},{5,1},{6,2},{7,3},{8,12},{9,13},{10,... | collective-permute-start | bytes 61448 | tf_op jit(solution)/shard_map/ppermute | solution.py:321
  22.4 5.8 %collective-permute-start.7 = (bf16[1,80,128]{2,1,0:T(8,128)(2,1)S(1)}, bf16[1,80,128]{2,1,0:T(8,128)(2,1)S(1)}, u32[]{:S(2)}, u32[]{:S(2)}) collective-permute-start(bf16[1,80,128]{2,1,0:T(8,128)(2,1)S(1)} %get-tuple-element.29.after_ref), channel_id=1, source_target_pairs={{0,2},{1,3},{2,0},{3,1},{4,6},{5,7},{6,4},{7,5},{8,10},{9,11},{10,... | collective-permute-start | bytes 61448 | tf_op jit(solution)/shard_map/ppermute | solution.py:321
  31.2 5.1 %collective-permute-start.8 = (bf16[4,8,2048]{2,1,0:T(8,128)(2,1)S(1)}, bf16[4,8,2048]{2,1,0:T(8,128)(2,1)S(1)}, u32[]{:S(2)}, u32[]{:S(2)}) collective-permute-start(bf16[4,8,2048]{2,1,0:T(8,128)(2,1)S(1)} %get-tuple-element.33), channel_id=1, source_target_pairs={{0,1},{1,0},{2,3},{3,2},{4,5},{5,4},{6,7},{7,6},{8,9},{9,8},{10,11... | collective-permute-start | bytes 393224 | tf_op jit(solution)/shard_map/ppermute | solution.py:321
  32.3 4.0 %copy-start = (bf16[1,8,2048]{2,1,0:T(8,128)(2,1)S(1)}, bf16[1,8,2048]{2,1,0:T(8,128)(2,1)}, u32[]{:S(2)}) copy-start(bf16[1,8,2048]{2,1,0:T(8,128)(2,1)} %residual_ref.1) | copy-start | bytes 98308
  36.3 6.2 %collective-permute-start.9 = (bf16[2,8,2048]{2,1,0:T(8,128)(2,1)S(1)}, bf16[2,8,2048]{2,1,0:T(8,128)(2,1)S(1)}, u32[]{:S(2)}, u32[]{:S(2)}) collective-permute-start(bf16[2,8,2048]{2,1,0:T(8,128)(2,1)S(1)} %get-tuple-element.34), channel_id=1, source_target_pairs={{0,6},{1,7},{2,4},{3,5},{4,2},{5,3},{6,0},{7,1},{8,14},{9,15},{10,... | collective-permute-start | bytes 196616 | tf_op jit(solution)/shard_map/ppermute | solution.py:321
  38.3 5.6 %collective-permute-start.11 = (bf16[2,8,2048]{2,1,0:T(8,128)(2,1)S(1)}, bf16[2,8,2048]{2,1,0:T(8,128)(2,1)S(1)}, u32[]{:S(2)}, u32[]{:S(2)}) collective-permute-start(bf16[2,8,2048]{2,1,0:T(8,128)(2,1)S(1)} %get-tuple-element.36), channel_id=1, source_target_pairs={{0,2},{1,3},{2,0},{3,1},{4,6},{5,7},{6,4},{7,5},{8,10},{9,11},{10,... | collective-permute-start | bytes 196616 | tf_op jit(solution)/shard_map/ppermute | solution.py:321
  38.3 5.6 %collective-permute-start.10 = (bf16[2,8,2048]{2,1,0:T(8,128)(2,1)S(1)}, bf16[2,8,2048]{2,1,0:T(8,128)(2,1)S(1)}, u32[]{:S(2)}, u32[]{:S(2)}) collective-permute-start(bf16[2,8,2048]{2,1,0:T(8,128)(2,1)S(1)} %get-tuple-element.35.near_ref), channel_id=1, source_target_pairs={{0,4},{1,5},{2,6},{3,7},{4,0},{5,1},{6,2},{7,3},{8,12},{9,13},{10,... | collective-permute-start | bytes 196616 | tf_op jit(solution)/shard_map/ppermute | solution.py:321
  44.0 5.0 %collective-permute-start.15 = (bf16[2,8,2048]{2,1,0:T(8,128)(2,1)S(1)}, bf16[2,8,2048]{2,1,0:T(8,128)(2,1)S(1)}, u32[]{:S(2)}, u32[]{:S(2)}) collective-permute-start(bf16[2,8,2048]{2,1,0:T(8,128)(2,1)S(1)} %owner.1), channel_id=1, source_target_pairs={{0,11},{1,10},{2,9},{3,8},{4,15},{5,14},{6,13},{7,12},{8,3},{9,2},... | collective-permute-start | bytes 196616 | tf_op jit(solution)/shard_map/ppermute | solution.py:321
  44.1 5.2 %collective-permute-start.14 = (bf16[2,8,2048]{2,1,0:T(8,128)(2,1)S(1)}, bf16[2,8,2048]{2,1,0:T(8,128)(2,1)S(1)}, u32[]{:S(2)}, u32[]{:S(2)}) collective-permute-start(bf16[2,8,2048]{2,1,0:T(8,128)(2,1)S(1)} %owner.1), channel_id=1, source_target_pairs={{0,10},{1,11},{2,8},{3,9},{4,14},{5,15},{6,12},{7,13},{8,2},{9,3},... | collective-permute-start | bytes 196616 | tf_op jit(solution)/shard_map/ppermute | solution.py:321
  46.3 4.3 %collective-permute-start.13 = (bf16[2,8,2048]{2,1,0:T(8,128)(2,1)S(1)}, bf16[2,8,2048]{2,1,0:T(8,128)(2,1)S(1)}, u32[]{:S(2)}, u32[]{:S(2)}) collective-permute-start(bf16[2,8,2048]{2,1,0:T(8,128)(2,1)S(1)} %owner.1), channel_id=1, source_target_pairs={{0,9},{1,8},{2,11},{3,10},{4,13},{5,12},{6,15},{7,14},{8,1},{9,0},... | collective-permute-start | bytes 196616 | tf_op jit(solution)/shard_map/ppermute | solution.py:321
  46.9 3.7 %collective-permute-start.12 = (bf16[2,8,2048]{2,1,0:T(8,128)(2,1)S(1)}, bf16[2,8,2048]{2,1,0:T(8,128)(2,1)S(1)}, u32[]{:S(2)}, u32[]{:S(2)}) collective-permute-start(bf16[2,8,2048]{2,1,0:T(8,128)(2,1)S(1)} %owner.1), channel_id=1, source_target_pairs={{0,8},{1,9},{2,10},{3,11},{4,12},{5,13},{6,14},{7,15},{8,0},{9,1},... | collective-permute-start | bytes 196616 | tf_op jit(solution)/shard_map/ppermute | solution.py:321

commit v3 on v2

--- a/solution.py
+++ b/solution.py
@@ -141,16 +141,17 @@
 
 def attention_kernel(stored_ref, limit_ref, after_ref, *refs):
     del after_ref
-    sources, outs, (scores_ref, mixed_ref) = refs[:4], refs[4:6], refs[6:]
-    quarter, rows, heads, dim = sources[0].shape
-    tp = 4 * quarter
+    sources, outs, (scores_ref, mixed_ref) = refs[:2], refs[2:4], refs[4:]
+    half, rows, heads, dim = sources[0].shape
+    tp = 2 * half
     kv_heads, span = stored_ref.shape[2:4]
     group = heads * tp // kv_heads
     per = group // heads
     scale = 1.0 / math.sqrt(dim)
 
     def query(k, r):
-        return sources[k // quarter][k % quarter, r].astype(F32)
+        array, at = place(k, tp)
+        return sources[array][at, r].astype(F32)
 
     for m in range(kv_heads):
         for r in range(rows):
@@ -348,7 +349,7 @@
         staged.append((units, held))
         return held
 
-    got = exchanged(queries, 1)
+    got = [exchanged(queries, k) for k in groups[::-1]]
     units = next_units(2)
     stored, limit, have, held = call(
         functools.partial(stage_cache_kernel, tp // kv_heads, units),
@@ -371,24 +372,19 @@
         cost=8 * MIB,
     )
     staged.append((units, held))
-    after = limit
+    have, after = [have, *got], limit
     for b in range(bits - 2):
-        count = 2 << b
-        have = call(
-            append_kernel, "append", struct((count, rows, heads, dim), BF16), (after, have, got)
-        )
-        after = have
-        if b < bits - 3:
-            got = exchanged(have, 2 << b)
-    all_queries = [have, *(exchanged(have, k) for k in reversed(groups))]
-    all_queries[1:] = all_queries[:0:-1]
-    after = stage(have, 2)
+        after = call(
+            append_kernel, "append", struct((4 << b, rows, heads, dim), BF16), (after, *have)
+        )
+        have = [after, exchanged(after, 1 << b)]
+    after = stage(after, 3)
     packed_block = (heads * rows + STAT_ROWS, dim)
     kept, send = call(
         attention_kernel,
         "attention",
         [struct((half, *packed_block), BF16)] * 2,
-        (stored, limit, after, *all_queries),
+        (stored, limit, after, *have),
         scratch=[pltpu.VMEM((heads * tp, rows, span), F32)] * 2,
         cost=8 * MIB,
     )
@@ -405,7 +401,7 @@
     )
     last = pending[3]
     pending = [pending[0], *(exchanged(block, k) for block, k in zip(pending[1:], groups[::-1]))]
-    stage(last, 4)
+    stage(last, 3)
 
     held = [array for _, array in staged]
     places = [(a, i) for a, (units, _) in enumerate(staged) for i in range(len(units))]

time: 51.4 us -> 51.9 us (level)
  Pallas kernels: 21.3 us -> 22.1 us
    pallas_call x12, Pallas kernels: 21.3 us -> 22.1 us  [call(): pl.pallas_call(kernel, out_shape=outs, in_specs=in_specs or [VMEM_SPEC] *...]
  transfers between devices with their start and end apart: 16 -> 16, of which waited for: 6 -> 11; matrix products, arithmetic and copies ran while one was open for 0% -> 0% of each run, Pallas kernels for 32% -> 31%
where the time goes in v3:
time: 51.9 us; the launch traced here: 51.8 us
  Pallas kernels  22.1 us (43%)
  starting transfers between devices  21.8 us (42%)
  waiting for transfers between devices  7.81 us (15%)
    pallas_call x12, Pallas kernels, call(): pl.pallas_call(kernel, out_shape=outs, in_specs=in_specs or [VMEM_SPEC] *...  22.1 us
    ppermute x16, starting transfers between devices, exchanged(): return lax.ppermute(array, ('section', 'tp'), pairs)  21.8 us
    ppermute x16, waiting for transfers between devices, exchanged(): return lax.ppermute(array, ('section', 'tp'), pairs)  7.81 us
  transfers between devices with their start and end apart: 16, of which 11 were waited for; matrix products, arithmetic and copies ran while one was open for 0% of the time, Pallas kernels for 31%

profile of v3, /device:TPU:0, one launch (start us, length us, event | category | flops | bytes accessed | tf_op | source)
XLA Modules:
  0.0 51.8 jit_solution(2564649130235743458)
XLA Ops:
  0.0 5.0 %collective-permute-start = (bf16[1,8,8,128]{3,2,1,0:T(8,128)(2,1)}, bf16[1,8,8,128]{3,2,1,0:T(8,128)(2,1)S(1)}, u32[]{:S(2)}, u32[]{:S(2)}) collective-permute-start(bf16[1,8,8,128]{3,2,1,0:T(8,128)(2,1)} %queries_ref.1), channel_id=1, source_target_pairs={{0,6},{1,7},{2,4},{3,5},{4,2},{5,3},{6,0},{7,1},{8,14},{9,15},{10,... | collective-permute-start | bytes 49160 | tf_op jit(solution)/shard_map/ppermute | solution.py:322
  5.6 2.9 %stage_cache.1 = (bf16[8,2,4,128,128]{4,3,2,1,0:T(8,128)(2,1)S(1)}, s32[8,128]{1,0:T(8,128)S(1)}, bf16[1,8,8,128]{3,2,1,0:T(8,128)(2,1)S(1)}, bf16[2,1024,1024]{2,1,0:T(8,128)(2,1)S(1)}) custom-call(s32[1,8]{1,0:T(1,128)} %lengths_ref.1, bf16[1,8,2,4,128]{4,3,2,1,0:T(4,128)(2,1)} %new_ref.1, bf16[1,8,2,4,128,128]{5,4,3,2,1,0:T(8,128)(2,1)} %kv_ref.1, ...), custom_call_target="tpu_custom_call" | custom-call | flops 8388608 | bytes 8388608 | tf_op jit(solution)/shard_map/stage_cache/pallas_call | solution.py:291
  9.0 0.9 %collective-permute-done.1.refs_2_ = bf16[1,8,8,128]{3,2,1,0:T(8,128)(2,1)S(1)} collective-permute-done((bf16[1,8,8,128]{3,2,1,0:T(8,128)(2,1)}, bf16[1,8,8,128]{3,2,1,0:T(8,128)(2,1)S(1)}, u32[]{:S(2)}, u32[]{:S(2)}) %collective-permute-start.1) | collective-permute-done | bytes 16416 | tf_op jit(solution)/shard_map/ppermute | solution.py:322
  9.9 1.5 %collective-permute-start.3 = (bf16[4,8,8,128]{3,2,1,0:T(8,128)(2,1)S(1)}, bf16[4,8,8,128]{3,2,1,0:T(8,128)(2,1)S(1)}, u32[]{:S(2)}, u32[]{:S(2)}) collective-permute-start(bf16[4,8,8,128]{3,2,1,0:T(8,128)(2,1)S(1)} %append.1.after_ref.refs_0_), channel_id=1, source_target_pairs={{0,1},{1,0},{2,3},{3,2},{4,5},{5,4},{6,7},{7,6},{8,9},{9,8},{10,11... | collective-permute-start | bytes 196616 | tf_op jit(solution)/shard_map/ppermute | solution.py:322
  11.4 2.9 %stage.3.after_ref.refs_6_.refs_1_ = bf16[3,1024,1024]{2,1,0:T(8,128)(2,1)S(1)} custom-call(bf16[1,1024,16384]{2,1,0:T(8,128)(2,1)} %weight_ref.9, bf16[4,8,8,128]{3,2,1,0:T(8,128)(2,1)S(1)} %append.1.after_ref.refs_0_), custom_call_target="tpu_custom_call" | custom-call | flops 6291456 | bytes 6291456 | tf_op jit(solution)/shard_map/stage/pallas_call | solution.py:291
  14.3 1.1 %attention.1 = (bf16[4,80,128]{2,1,0:T(8,128)(2,1)S(1)}, bf16[4,80,128]{2,1,0:T(8,128)(2,1)S(1)}) custom-call(bf16[8,2,4,128,128]{4,3,2,1,0:T(8,128)(2,1)S(1)} %get-tuple-element.21.stored_ref, s32[8,128]{1,0:T(8,128)S(1)} %get-tuple-element.22.after_ref.limit_ref, bf16[3,1024,1024]{2,1,0:T(8,128)(2,1)S(1)} %stage.3.after_ref.refs_6_.refs_1_, ...), custom_call_target="tpu_custom_call" | custom-call | flops 8388608 | bytes 8388608 | tf_op jit(solution)/shard_map/attention/pallas_call | solution.py:291
  15.5 1.4 %collective-permute-start.4 = (bf16[4,80,128]{2,1,0:T(8,128)(2,1)S(1)}, bf16[4,80,128]{2,1,0:T(8,128)(2,1)S(1)}, u32[]{:S(2)}, u32[]{:S(2)}) collective-permute-start(bf16[4,80,128]{2,1,0:T(8,128)(2,1)S(1)} %get-tuple-element.24.after_ref), channel_id=1, source_target_pairs={{0,1},{1,0},{2,3},{3,2},{4,5},{5,4},{6,7},{7,6},{8,9},{9,8},{10,11... | collective-permute-start | bytes 245768 | tf_op jit(solution)/shard_map/ppermute | solution.py:322
  16.9 3.5 %stage.4.after_ref.refs_7_.refs_2_ = bf16[4,1024,1024]{2,1,0:T(8,128)(2,1)S(1)} custom-call(bf16[1,1024,16384]{2,1,0:T(8,128)(2,1)} %weight_ref.9, bf16[4,80,128]{2,1,0:T(8,128)(2,1)S(1)} %get-tuple-element.24.after_ref), custom_call_target="tpu_custom_call" | custom-call | flops 8388608 | bytes 8388608 | tf_op jit(solution)/shard_map/stage/pallas_call | solution.py:291
  20.6 2.7 %collective-permute-start.5 = (bf16[1,80,128]{2,1,0:T(8,128)(2,1)S(1)}, bf16[1,80,128]{2,1,0:T(8,128)(2,1)S(1)}, u32[]{:S(2)}, u32[]{:S(2)}) collective-permute-start(bf16[1,80,128]{2,1,0:T(8,128)(2,1)S(1)} %get-tuple-element.27), channel_id=1, source_target_pairs={{0,6},{1,7},{2,4},{3,5},{4,2},{5,3},{6,0},{7,1},{8,14},{9,15},{10,... | collective-permute-start | bytes 61448 | tf_op jit(solution)/shard_map/ppermute | solution.py:322
  23.2 0.9 %collective-permute-start.6 = (bf16[1,80,128]{2,1,0:T(8,128)(2,1)S(1)}, bf16[1,80,128]{2,1,0:T(8,128)(2,1)S(1)}, u32[]{:S(2)}, u32[]{:S(2)}) collective-permute-start(bf16[1,80,128]{2,1,0:T(8,128)(2,1)S(1)} %get-tuple-element.28), channel_id=1, source_target_pairs={{0,4},{1,5},{2,6},{3,7},{4,0},{5,1},{6,2},{7,3},{8,12},{9,13},{10,... | collective-permute-start | bytes 61448 | tf_op jit(solution)/shard_map/ppermute | solution.py:322
  24.1 0.9 %collective-permute-start.7 = (bf16[1,80,128]{2,1,0:T(8,128)(2,1)S(1)}, bf16[1,80,128]{2,1,0:T(8,128)(2,1)S(1)}, u32[]{:S(2)}, u32[]{:S(2)}) collective-permute-start(bf16[1,80,128]{2,1,0:T(8,128)(2,1)S(1)} %get-tuple-element.29.after_ref), channel_id=1, source_target_pairs={{0,2},{1,3},{2,0},{3,1},{4,6},{5,7},{6,4},{7,5},{8,10},{9,11},{10,... | collective-permute-start | bytes 61448 | tf_op jit(solution)/shard_map/ppermute | solution.py:322
  25.0 2.9 %stage.5.refs_8_.refs_3_ = bf16[3,1024,1024]{2,1,0:T(8,128)(2,1)S(1)} custom-call(bf16[1,1024,16384]{2,1,0:T(8,128)(2,1)} %weight_ref.9, bf16[1,80,128]{2,1,0:T(8,128)(2,1)S(1)} %get-tuple-element.29.after_ref), custom_call_target="tpu_custom_call" | custom-call | flops 6291456 | bytes 6291456 | tf_op jit(solution)/shard_map/stage/pallas_call | solution.py:291
  28.1 3.7 %project_away.1 = (bf16[8,1024]{1,0:T(8,128)(2,1)S(1)}, bf16[4,8,2048]{2,1,0:T(8,128)(2,1)S(1)}, bf16[2,1024,1024]{2,1,0:T(8,128)(2,1)S(1)}) custom-call(bf16[1,80,128]{2,1,0:T(8,128)(2,1)S(1)} %get-tuple-element.26.refs_0_, bf16[1,80,128]{2,1,0:T(8,128)(2,1)S(1)} %collective-permute-done.5.refs_1_, bf16[1,80,128]{2,1,0:T(8,128)(2,1)S(1)} %collective-permute-done.6.refs_2_, ...), custom_call_target="tpu_custom_call" | custom-call | flops 16777216 | bytes 16777216 | tf_op jit(solution)/shard_map/project_away/pallas_call | solution.py:291
  31.8 1.0 %collective-permute-start.8 = (bf16[4,8,2048]{2,1,0:T(8,128)(2,1)S(1)}, bf16[4,8,2048]{2,1,0:T(8,128)(2,1)S(1)}, u32[]{:S(2)}, u32[]{:S(2)}) collective-permute-start(bf16[4,8,2048]{2,1,0:T(8,128)(2,1)S(1)} %get-tuple-element.33), channel_id=1, source_target_pairs={{0,1},{1,0},{2,3},{3,2},{4,5},{5,4},{6,7},{7,6},{8,9},{9,8},{10,11... | collective-permute-start | bytes 393224 | tf_op jit(solution)/shard_map/ppermute | solution.py:322
  32.8 3.9 %project_own.1.kept_ref = f32[4,8,2048]{2,1,0:T(8,128)S(1)} custom-call(bf16[8,1024]{1,0:T(8,128)(2,1)S(1)} %get-tuple-element.31.flat_ref, bf16[1,1024,16384]{2,1,0:T(8,128)(2,1)} %weight_ref.9, bf16[2,1024,1024]{2,1,0:T(8,128)(2,1)S(1)} %get-tuple-element.30.refs_5_.refs_0_, bf16[3,1024,1024]{2,1,0:T(8,128)(2,1)S(1)} %stage.3.after_ref.refs_6_.refs_1_, ...), custom_call_target="tpu_custom_call" | custom-call | flops 16777216 | bytes 16777216 | tf_op jit(solution)/shard_map/project_own/pallas_call | solution.py:291
  36.9 2.5 %collective-permute-start.9 = (bf16[2,8,2048]{2,1,0:T(8,128)(2,1)S(1)}, bf16[2,8,2048]{2,1,0:T(8,128)(2,1)S(1)}, u32[]{:S(2)}, u32[]{:S(2)}) collective-permute-start(bf16[2,8,2048]{2,1,0:T(8,128)(2,1)S(1)} %get-tuple-element.34), channel_id=1, source_target_pairs={{0,6},{1,7},{2,4},{3,5},{4,2},{5,3},{6,0},{7,1},{8,14},{9,15},{10,... | collective-permute-start | bytes 196616 | tf_op jit(solution)/shard_map/ppermute | solution.py:322
  39.4 1.9 %collective-permute-start.10 = (bf16[2,8,2048]{2,1,0:T(8,128)(2,1)S(1)}, bf16[2,8,2048]{2,1,0:T(8,128)(2,1)S(1)}, u32[]{:S(2)}, u32[]{:S(2)}) collective-permute-start(bf16[2,8,2048]{2,1,0:T(8,128)(2,1)S(1)} %get-tuple-element.35.near_ref), channel_id=1, source_target_pairs={{0,4},{1,5},{2,6},{3,7},{4,0},{5,1},{6,2},{7,3},{8,12},{9,13},{10,... | collective-permute-start | bytes 196616 | tf_op jit(solution)/shard_map/ppermute | solution.py:322
  41.3 1.7 %collective-permute-done.9.three_ref = bf16[2,8,2048]{2,1,0:T(8,128)(2,1)S(1)} collective-permute-done((bf16[2,8,2048]{2,1,0:T(8,128)(2,1)S(1)}, bf16[2,8,2048]{2,1,0:T(8,128)(2,1)S(1)}, u32[]{:S(2)}, u32[]{:S(2)}) %collective-permute-start.9) | collective-permute-done | bytes 65568 | tf_op jit(solution)/shard_map/ppermute | solution.py:322
  43.7 0.8 %collective-permute-done.10.two_ref = bf16[2,8,2048]{2,1,0:T(8,128)(2,1)S(1)} collective-permute-done((bf16[2,8,2048]{2,1,0:T(8,128)(2,1)S(1)}, bf16[2,8,2048]{2,1,0:T(8,128)(2,1)S(1)}, u32[]{:S(2)}, u32[]{:S(2)}) %collective-permute-start.10) | collective-permute-done | bytes 65568 | tf_op jit(solution)/shard_map/ppermute | solution.py:322
  44.8 2.2 %collective-permute-start.14 = (bf16[2,8,2048]{2,1,0:T(8,128)(2,1)S(1)}, bf16[2,8,2048]{2,1,0:T(8,128)(2,1)S(1)}, u32[]{:S(2)}, u32[]{:S(2)}) collective-permute-start(bf16[2,8,2048]{2,1,0:T(8,128)(2,1)S(1)} %owner.1), channel_id=1, source_target_pairs={{0,10},{1,11},{2,8},{3,9},{4,14},{5,15},{6,12},{7,13},{8,2},{9,3},... | collective-permute-start | bytes 196616 | tf_op jit(solution)/shard_map/ppermute | solution.py:322
  47.0 1.0 %collective-permute-start.13 = (bf16[2,8,2048]{2,1,0:T(8,128)(2,1)S(1)}, bf16[2,8,2048]{2,1,0:T(8,128)(2,1)S(1)}, u32[]{:S(2)}, u32[]{:S(2)}) collective-permute-start(bf16[2,8,2048]{2,1,0:T(8,128)(2,1)S(1)} %owner.1), channel_id=1, source_target_pairs={{0,9},{1,8},{2,11},{3,10},{4,13},{5,12},{6,15},{7,14},{8,1},{9,0},... | collective-permute-start | bytes 196616 | tf_op jit(solution)/shard_map/ppermute | solution.py:322
  48.1 1.8 %collective-permute-done.15.refs_3_ = bf16[2,8,2048]{2,1,0:T(8,128)(2,1)S(1)} collective-permute-done((bf16[2,8,2048]{2,1,0:T(8,128)(2,1)S(1)}, bf16[2,8,2048]{2,1,0:T(8,128)(2,1)S(1)}, u32[]{:S(2)}, u32[]{:S(2)}) %collective-permute-start.15) | collective-permute-done | bytes 65568 | tf_op jit(solution)/shard_map/ppermute | solution.py:322
  50.3 0.7 %collective-permute-done.13.refs_1_ = bf16[2,8,2048]{2,1,0:T(8,128)(2,1)S(1)} collective-permute-done((bf16[2,8,2048]{2,1,0:T(8,128)(2,1)S(1)}, bf16[2,8,2048]{2,1,0:T(8,128)(2,1)S(1)}, u32[]{:S(2)}, u32[]{:S(2)}) %collective-permute-start.13) | collective-permute-done | bytes 65568 | tf_op jit(solution)/shard_map/ppermute | solution.py:322
  51.0 0.7 %placed.1 = bf16[1,8,16384]{2,1,0:T(8,128)(2,1)} custom-call(bf16[2,8,2048]{2,1,0:T(8,128)(2,1)S(1)} %collective-permute-done.12.refs_0_, bf16[2,8,2048]{2,1,0:T(8,128)(2,1)S(1)} %collective-permute-done.13.refs_1_, bf16[2,8,2048]{2,1,0:T(8,128)(2,1)S(1)} %collective-permute-done.14.refs_2_, bf16[2,8,2048]{2,1,0:T(8,128)(2,1)S(1)} %collective-permute-done.15.refs_3_), custom_call_target="tpu_custom_call" | custom-call | flops 1048576 | bytes 1048576 | tf_op jit(solution)/shard_map/placed/pallas_call | solution.py:291
  (22 shorter events, 2.9 us)
Async XLA Ops:
  0.0 8.6 %collective-permute-start = (bf16[1,8,8,128]{3,2,1,0:T(8,128)(2,1)}, bf16[1,8,8,128]{3,2,1,0:T(8,128)(2,1)S(1)}, u32[]{:S(2)}, u32[]{:S(2)}) collective-permute-start(bf16[1,8,8,128]{3,2,1,0:T(8,128)(2,1)} %queries_ref.1), channel_id=1, source_target_pairs={{0,6},{1,7},{2,4},{3,5},{4,2},{5,3},{6,0},{7,1},{8,14},{9,15},{10,... | collective-permute-start | bytes 49160 | tf_op jit(solution)/shard_map/ppermute | solution.py:322
  5.0 3.9 %collective-permute-start.2 = (bf16[1,8,8,128]{3,2,1,0:T(8,128)(2,1)}, bf16[1,8,8,128]{3,2,1,0:T(8,128)(2,1)S(1)}, u32[]{:S(2)}, u32[]{:S(2)}) collective-permute-start(bf16[1,8,8,128]{3,2,1,0:T(8,128)(2,1)} %queries_ref.1), channel_id=1, source_target_pairs={{0,2},{1,3},{2,0},{3,1},{4,6},{5,7},{6,4},{7,5},{8,10},{9,11},{10,... | collective-permute-start | bytes 49160 | tf_op jit(solution)/shard_map/ppermute | solution.py:322
  5.1 4.8 %collective-permute-start.1 = (bf16[1,8,8,128]{3,2,1,0:T(8,128)(2,1)}, bf16[1,8,8,128]{3,2,1,0:T(8,128)(2,1)S(1)}, u32[]{:S(2)}, u32[]{:S(2)}) collective-permute-start(bf16[1,8,8,128]{3,2,1,0:T(8,128)(2,1)} %queries_ref.1), channel_id=1, source_target_pairs={{0,4},{1,5},{2,6},{3,7},{4,0},{5,1},{6,2},{7,3},{8,12},{9,13},{10,... | collective-permute-start | bytes 49160 | tf_op jit(solution)/shard_map/ppermute | solution.py:322
  9.9 4.4 %collective-permute-start.3 = (bf16[4,8,8,128]{3,2,1,0:T(8,128)(2,1)S(1)}, bf16[4,8,8,128]{3,2,1,0:T(8,128)(2,1)S(1)}, u32[]{:S(2)}, u32[]{:S(2)}) collective-permute-start(bf16[4,8,8,128]{3,2,1,0:T(8,128)(2,1)S(1)} %append.1.after_ref.refs_0_), channel_id=1, source_target_pairs={{0,1},{1,0},{2,3},{3,2},{4,5},{5,4},{6,7},{7,6},{8,9},{9,8},{10,11... | collective-permute-start | bytes 196616 | tf_op jit(solution)/shard_map/ppermute | solution.py:322
  15.5 4.9 %collective-permute-start.4 = (bf16[4,80,128]{2,1,0:T(8,128)(2,1)S(1)}, bf16[4,80,128]{2,1,0:T(8,128)(2,1)S(1)}, u32[]{:S(2)}, u32[]{:S(2)}) collective-permute-start(bf16[4,80,128]{2,1,0:T(8,128)(2,1)S(1)} %get-tuple-element.24.after_ref), channel_id=1, source_target_pairs={{0,1},{1,0},{2,3},{3,2},{4,5},{5,4},{6,7},{7,6},{8,9},{9,8},{10,11... | collective-permute-start | bytes 245768 | tf_op jit(solution)/shard_map/ppermute | solution.py:322
  20.6 7.4 %collective-permute-start.5 = (bf16[1,80,128]{2,1,0:T(8,128)(2,1)S(1)}, bf16[1,80,128]{2,1,0:T(8,128)(2,1)S(1)}, u32[]{:S(2)}, u32[]{:S(2)}) collective-permute-start(bf16[1,80,128]{2,1,0:T(8,128)(2,1)S(1)} %get-tuple-element.27), channel_id=1, source_target_pairs={{0,6},{1,7},{2,4},{3,5},{4,2},{5,3},{6,0},{7,1},{8,14},{9,15},{10,... | collective-permute-start | bytes 61448 | tf_op jit(solution)/shard_map/ppermute | solution.py:322
  23.2 4.8 %collective-permute-start.6 = (bf16[1,80,128]{2,1,0:T(8,128)(2,1)S(1)}, bf16[1,80,128]{2,1,0:T(8,128)(2,1)S(1)}, u32[]{:S(2)}, u32[]{:S(2)}) collective-permute-start(bf16[1,80,128]{2,1,0:T(8,128)(2,1)S(1)} %get-tuple-element.28), channel_id=1, source_target_pairs={{0,4},{1,5},{2,6},{3,7},{4,0},{5,1},{6,2},{7,3},{8,12},{9,13},{10,... | collective-permute-start | bytes 61448 | tf_op jit(solution)/shard_map/ppermute | solution.py:322
  24.1 4.0 %collective-permute-start.7 = (bf16[1,80,128]{2,1,0:T(8,128)(2,1)S(1)}, bf16[1,80,128]{2,1,0:T(8,128)(2,1)S(1)}, u32[]{:S(2)}, u32[]{:S(2)}) collective-permute-start(bf16[1,80,128]{2,1,0:T(8,128)(2,1)S(1)} %get-tuple-element.29.after_ref), channel_id=1, source_target_pairs={{0,2},{1,3},{2,0},{3,1},{4,6},{5,7},{6,4},{7,5},{8,10},{9,11},{10,... | collective-permute-start | bytes 61448 | tf_op jit(solution)/shard_map/ppermute | solution.py:322
  31.8 5.0 %collective-permute-start.8 = (bf16[4,8,2048]{2,1,0:T(8,128)(2,1)S(1)}, bf16[4,8,2048]{2,1,0:T(8,128)(2,1)S(1)}, u32[]{:S(2)}, u32[]{:S(2)}) collective-permute-start(bf16[4,8,2048]{2,1,0:T(8,128)(2,1)S(1)} %get-tuple-element.33), channel_id=1, source_target_pairs={{0,1},{1,0},{2,3},{3,2},{4,5},{5,4},{6,7},{7,6},{8,9},{9,8},{10,11... | collective-permute-start | bytes 393224 | tf_op jit(solution)/shard_map/ppermute | solution.py:322
  32.8 4.1 %copy-start = (bf16[1,8,2048]{2,1,0:T(8,128)(2,1)S(1)}, bf16[1,8,2048]{2,1,0:T(8,128)(2,1)}, u32[]{:S(2)}) copy-start(bf16[1,8,2048]{2,1,0:T(8,128)(2,1)} %residual_ref.1) | copy-start | bytes 98308
  36.9 6.1 %collective-permute-start.9 = (bf16[2,8,2048]{2,1,0:T(8,128)(2,1)S(1)}, bf16[2,8,2048]{2,1,0:T(8,128)(2,1)S(1)}, u32[]{:S(2)}, u32[]{:S(2)}) collective-permute-start(bf16[2,8,2048]{2,1,0:T(8,128)(2,1)S(1)} %get-tuple-element.34), channel_id=1, source_target_pairs={{0,6},{1,7},{2,4},{3,5},{4,2},{5,3},{6,0},{7,1},{8,14},{9,15},{10,... | collective-permute-start | bytes 196616 | tf_op jit(solution)/shard_map/ppermute | solution.py:322
  39.4 4.3 %collective-permute-start.11 = (bf16[2,8,2048]{2,1,0:T(8,128)(2,1)S(1)}, bf16[2,8,2048]{2,1,0:T(8,128)(2,1)S(1)}, u32[]{:S(2)}, u32[]{:S(2)}) collective-permute-start(bf16[2,8,2048]{2,1,0:T(8,128)(2,1)S(1)} %get-tuple-element.36), channel_id=1, source_target_pairs={{0,2},{1,3},{2,0},{3,1},{4,6},{5,7},{6,4},{7,5},{8,10},{9,11},{10,... | collective-permute-start | bytes 196616 | tf_op jit(solution)/shard_map/ppermute | solution.py:322
  39.4 5.2 %collective-permute-start.10 = (bf16[2,8,2048]{2,1,0:T(8,128)(2,1)S(1)}, bf16[2,8,2048]{2,1,0:T(8,128)(2,1)S(1)}, u32[]{:S(2)}, u32[]{:S(2)}) collective-permute-start(bf16[2,8,2048]{2,1,0:T(8,128)(2,1)S(1)} %get-tuple-element.35.near_ref), channel_id=1, source_target_pairs={{0,4},{1,5},{2,6},{3,7},{4,0},{5,1},{6,2},{7,3},{8,12},{9,13},{10,... | collective-permute-start | bytes 196616 | tf_op jit(solution)/shard_map/ppermute | solution.py:322
  44.7 5.2 %collective-permute-start.15 = (bf16[2,8,2048]{2,1,0:T(8,128)(2,1)S(1)}, bf16[2,8,2048]{2,1,0:T(8,128)(2,1)S(1)}, u32[]{:S(2)}, u32[]{:S(2)}) collective-permute-start(bf16[2,8,2048]{2,1,0:T(8,128)(2,1)S(1)} %owner.1), channel_id=1, source_target_pairs={{0,11},{1,10},{2,9},{3,8},{4,15},{5,14},{6,13},{7,12},{8,3},{9,2},... | collective-permute-start | bytes 196616 | tf_op jit(solution)/shard_map/ppermute | solution.py:322
  44.8 5.5 %collective-permute-start.14 = (bf16[2,8,2048]{2,1,0:T(8,128)(2,1)S(1)}, bf16[2,8,2048]{2,1,0:T(8,128)(2,1)S(1)}, u32[]{:S(2)}, u32[]{:S(2)}) collective-permute-start(bf16[2,8,2048]{2,1,0:T(8,128)(2,1)S(1)} %owner.1), channel_id=1, source_target_pairs={{0,10},{1,11},{2,8},{3,9},{4,14},{5,15},{6,12},{7,13},{8,2},{9,3},... | collective-permute-start | bytes 196616 | tf_op jit(solution)/shard_map/ppermute | solution.py:322
  47.0 4.1 %collective-permute-start.13 = (bf16[2,8,2048]{2,1,0:T(8,128)(2,1)S(1)}, bf16[2,8,2048]{2,1,0:T(8,128)(2,1)S(1)}, u32[]{:S(2)}, u32[]{:S(2)}) collective-permute-start(bf16[2,8,2048]{2,1,0:T(8,128)(2,1)S(1)} %owner.1), channel_id=1, source_target_pairs={{0,9},{1,8},{2,11},{3,10},{4,13},{5,12},{6,15},{7,14},{8,1},{9,0},... | collective-permute-start | bytes 196616 | tf_op jit(solution)/shard_map/ppermute | solution.py:322
  48.0 3.0 %collective-permute-start.12 = (bf16[2,8,2048]{2,1,0:T(8,128)(2,1)S(1)}, bf16[2,8,2048]{2,1,0:T(8,128)(2,1)S(1)}, u32[]{:S(2)}, u32[]{:S(2)}) collective-permute-start(bf16[2,8,2048]{2,1,0:T(8,128)(2,1)S(1)} %owner.1), channel_id=1, source_target_pairs={{0,8},{1,9},{2,10},{3,11},{4,12},{5,13},{6,14},{7,15},{8,0},{9,1},... | collective-permute-start | bytes 196616 | tf_op jit(solution)/shard_map/ppermute | solution.py:322

commit v4 on v2

--- a/solution.py
+++ b/solution.py
@@ -255,7 +255,7 @@
         keep_ref[i] = kept_ref[2 * i] + got_ref[2 * i].astype(F32)
 
 
-def pair_kernel(kept_ref, got_ref, residual_ref, far_ref, even_ref, odd_ref):
+def pair_kernel(kept_ref, got_ref, residual_ref, far_ref, even_ref, odd_ref, near_ref):
     for i in range(4):
         x = kept_ref[i] + got_ref[i].astype(F32)
         if i == 0:
@@ -265,6 +265,7 @@
             far_ref[i >> 1] = x.astype(BF16)
         else:
             even_ref[i >> 1] = x.astype(BF16)
+            near_ref[i >> 1] = x.astype(BF16)
 
 
 def owner_kernel(three_ref, two_ref, one_ref, near_ref, out_ref):
@@ -445,14 +446,14 @@
             (kept, got),
         )
         got = exchanged(send, 1 << b)
-    far, even, odd = call(
-        pair_kernel, "pair_sum", [struct((2, rows, width), BF16)] * 3, (kept, got, residual)
+    far, even, odd, near = call(
+        pair_kernel, "pair_sum", [struct((2, rows, width), BF16)] * 4, (kept, got, residual)
     )
     three = exchanged(far, groups[2])
     two = exchanged(even, groups[1])
     one = exchanged(odd, groups[0])
     own = call(
-        owner_kernel, "owner", struct((2, rows, width), BF16), (three, two, one, even)
+        owner_kernel, "owner", struct((2, rows, width), BF16), (three, two, one, near)
     )
     high = 1 << (bits - 1)
     parts = [(k, exchanged(own, k, 1)) for k in range(high)]

time: 51.4 us -> 51.3 us (level)
  no operation moved by 1% of the time
where the time goes in v4:
time: 51.3 us; the launch traced here: 51.1 us
  starting transfers between devices  21.9 us (43%)
  Pallas kernels  21.3 us (42%)
  waiting for transfers between devices  7.85 us (15%)
    ppermute x16, starting transfers between devices, exchanged(): return lax.ppermute(array, ('section', 'tp'), pairs)  21.9 us
    pallas_call x12, Pallas kernels, call(): pl.pallas_call(kernel, out_shape=outs, in_specs=in_specs or [VMEM_SPEC] *...  21.3 us
    ppermute x16, waiting for transfers between devices, exchanged(): return lax.ppermute(array, ('section', 'tp'), pairs)  7.85 us
  transfers between devices with their start and end apart: 16, of which 6 were waited for; matrix products, arithmetic and copies ran while one was open for 0% of the time, Pallas kernels for 32%

profile of v4, /device:TPU:0, one launch (start us, length us, event | category | flops | bytes accessed | tf_op | source)
XLA Modules:
  0.0 51.1 jit_solution(7843800904940673025)
XLA Ops:
  0.0 3.0 %collective-permute-start = (bf16[1,8,8,128]{3,2,1,0:T(8,128)(2,1)}, bf16[1,8,8,128]{3,2,1,0:T(8,128)(2,1)S(1)}, u32[]{:S(2)}, u32[]{:S(2)}) collective-permute-start(bf16[1,8,8,128]{3,2,1,0:T(8,128)(2,1)} %queries_ref.1), channel_id=1, source_target_pairs={{0,1},{1,0},{2,3},{3,2},{4,5},{5,4},{6,7},{7,6},{8,9},{9,8},{10,11... | collective-permute-start | bytes 49160 | tf_op jit(solution)/shard_map/ppermute | solution.py:322
  3.0 2.9 %stage_cache.1 = (bf16[8,2,4,128,128]{4,3,2,1,0:T(8,128)(2,1)S(1)}, s32[8,128]{1,0:T(8,128)S(1)}, bf16[1,8,8,128]{3,2,1,0:T(8,128)(2,1)S(1)}, bf16[2,1024,1024]{2,1,0:T(8,128)(2,1)S(1)}) custom-call(s32[1,8]{1,0:T(1,128)} %lengths_ref.1, bf16[1,8,2,4,128]{4,3,2,1,0:T(4,128)(2,1)} %new_ref.1, bf16[1,8,2,4,128,128]{5,4,3,2,1,0:T(8,128)(2,1)} %kv_ref.1, ...), custom_call_target="tpu_custom_call" | custom-call | flops 8388608 | bytes 8388608 | tf_op jit(solution)/shard_map/stage_cache/pallas_call | solution.py:291
  5.9 3.7 %collective-permute-start.3 = (bf16[2,8,8,128]{3,2,1,0:T(8,128)(2,1)S(1)}, bf16[2,8,8,128]{3,2,1,0:T(8,128)(2,1)S(1)}, u32[]{:S(2)}, u32[]{:S(2)}) collective-permute-start(bf16[2,8,8,128]{3,2,1,0:T(8,128)(2,1)S(1)} %append.1.after_ref.refs_0_), channel_id=1, source_target_pairs={{0,6},{1,7},{2,4},{3,5},{4,2},{5,3},{6,0},{7,1},{8,14},{9,15},{10,... | collective-permute-start | bytes 98312 | tf_op jit(solution)/shard_map/ppermute | solution.py:322
  9.6 0.8 %collective-permute-start.1 = (bf16[2,8,8,128]{3,2,1,0:T(8,128)(2,1)S(1)}, bf16[2,8,8,128]{3,2,1,0:T(8,128)(2,1)S(1)}, u32[]{:S(2)}, u32[]{:S(2)}) collective-permute-start(bf16[2,8,8,128]{3,2,1,0:T(8,128)(2,1)S(1)} %append.1.after_ref.refs_0_), channel_id=1, source_target_pairs={{0,2},{1,3},{2,0},{3,1},{4,6},{5,7},{6,4},{7,5},{8,10},{9,11},{10,... | collective-permute-start | bytes 98312 | tf_op jit(solution)/shard_map/ppermute | solution.py:322
  10.4 2.2 %stage.3.after_ref.refs_6_.refs_1_ = bf16[2,1024,1024]{2,1,0:T(8,128)(2,1)S(1)} custom-call(bf16[1,1024,16384]{2,1,0:T(8,128)(2,1)} %weight_ref.9, bf16[2,8,8,128]{3,2,1,0:T(8,128)(2,1)S(1)} %append.1.after_ref.refs_0_), custom_call_target="tpu_custom_call" | custom-call | flops 4194304 | bytes 4194304 | tf_op jit(solution)/shard_map/stage/pallas_call | solution.py:291
  12.7 1.8 %collective-permute-done.2.refs_2_ = bf16[2,8,8,128]{3,2,1,0:T(8,128)(2,1)S(1)} collective-permute-done((bf16[2,8,8,128]{3,2,1,0:T(8,128)(2,1)S(1)}, bf16[2,8,8,128]{3,2,1,0:T(8,128)(2,1)S(1)}, u32[]{:S(2)}, u32[]{:S(2)}) %collective-permute-start.2) | collective-permute-done | bytes 32800 | tf_op jit(solution)/shard_map/ppermute | solution.py:322
  14.4 1.1 %attention.1 = (bf16[4,80,128]{2,1,0:T(8,128)(2,1)S(1)}, bf16[4,80,128]{2,1,0:T(8,128)(2,1)S(1)}) custom-call(bf16[8,2,4,128,128]{4,3,2,1,0:T(8,128)(2,1)S(1)} %get-tuple-element.22.stored_ref, s32[8,128]{1,0:T(8,128)S(1)} %get-tuple-element.23.after_ref.limit_ref, bf16[2,1024,1024]{2,1,0:T(8,128)(2,1)S(1)} %stage.3.after_ref.refs_6_.refs_1_, ...), custom_call_target="tpu_custom_call" | custom-call | flops 8388608 | bytes 8388608 | tf_op jit(solution)/shard_map/attention/pallas_call | solution.py:291
  15.5 1.0 %collective-permute-start.4 = (bf16[4,80,128]{2,1,0:T(8,128)(2,1)S(1)}, bf16[4,80,128]{2,1,0:T(8,128)(2,1)S(1)}, u32[]{:S(2)}, u32[]{:S(2)}) collective-permute-start(bf16[4,80,128]{2,1,0:T(8,128)(2,1)S(1)} %get-tuple-element.25.after_ref), channel_id=1, source_target_pairs={{0,1},{1,0},{2,3},{3,2},{4,5},{5,4},{6,7},{7,6},{8,9},{9,8},{10,11... | collective-permute-start | bytes 245768 | tf_op jit(solution)/shard_map/ppermute | solution.py:322
  16.5 3.5 %stage.4.after_ref.refs_7_.refs_2_ = bf16[4,1024,1024]{2,1,0:T(8,128)(2,1)S(1)} custom-call(bf16[1,1024,16384]{2,1,0:T(8,128)(2,1)} %weight_ref.9, bf16[4,80,128]{2,1,0:T(8,128)(2,1)S(1)} %get-tuple-element.25.after_ref), custom_call_target="tpu_custom_call" | custom-call | flops 8388608 | bytes 8388608 | tf_op jit(solution)/shard_map/stage/pallas_call | solution.py:291
  20.2 1.9 %collective-permute-start.5 = (bf16[1,80,128]{2,1,0:T(8,128)(2,1)S(1)}, bf16[1,80,128]{2,1,0:T(8,128)(2,1)S(1)}, u32[]{:S(2)}, u32[]{:S(2)}) collective-permute-start(bf16[1,80,128]{2,1,0:T(8,128)(2,1)S(1)} %get-tuple-element.28), channel_id=1, source_target_pairs={{0,6},{1,7},{2,4},{3,5},{4,2},{5,3},{6,0},{7,1},{8,14},{9,15},{10,... | collective-permute-start | bytes 61448 | tf_op jit(solution)/shard_map/ppermute | solution.py:322
  22.4 2.3 %collective-permute-start.7 = (bf16[1,80,128]{2,1,0:T(8,128)(2,1)S(1)}, bf16[1,80,128]{2,1,0:T(8,128)(2,1)S(1)}, u32[]{:S(2)}, u32[]{:S(2)}) collective-permute-start(bf16[1,80,128]{2,1,0:T(8,128)(2,1)S(1)} %get-tuple-element.30.after_ref), channel_id=1, source_target_pairs={{0,2},{1,3},{2,0},{3,1},{4,6},{5,7},{6,4},{7,5},{8,10},{9,11},{10,... | collective-permute-start | bytes 61448 | tf_op jit(solution)/shard_map/ppermute | solution.py:322
  24.7 3.5 %stage.5.refs_8_.refs_3_ = bf16[4,1024,1024]{2,1,0:T(8,128)(2,1)S(1)} custom-call(bf16[1,1024,16384]{2,1,0:T(8,128)(2,1)} %weight_ref.9, bf16[1,80,128]{2,1,0:T(8,128)(2,1)S(1)} %get-tuple-element.30.after_ref), custom_call_target="tpu_custom_call" | custom-call | flops 8388608 | bytes 8388608 | tf_op jit(solution)/shard_map/stage/pallas_call | solution.py:291
  28.2 2.9 %project_away.1 = (bf16[8,1024]{1,0:T(8,128)(2,1)S(1)}, bf16[4,8,2048]{2,1,0:T(8,128)(2,1)S(1)}, bf16[2,1024,1024]{2,1,0:T(8,128)(2,1)S(1)}) custom-call(bf16[1,80,128]{2,1,0:T(8,128)(2,1)S(1)} %get-tuple-element.27.refs_0_, bf16[1,80,128]{2,1,0:T(8,128)(2,1)S(1)} %collective-permute-done.5.refs_1_, bf16[1,80,128]{2,1,0:T(8,128)(2,1)S(1)} %collective-permute-done.6.refs_2_, ...), custom_call_target="tpu_custom_call" | custom-call | flops 16777216 | bytes 16777216 | tf_op jit(solution)/shard_map/project_away/pallas_call | solution.py:291
  31.2 1.2 %collective-permute-start.8 = (bf16[4,8,2048]{2,1,0:T(8,128)(2,1)S(1)}, bf16[4,8,2048]{2,1,0:T(8,128)(2,1)S(1)}, u32[]{:S(2)}, u32[]{:S(2)}) collective-permute-start(bf16[4,8,2048]{2,1,0:T(8,128)(2,1)S(1)} %get-tuple-element.34), channel_id=1, source_target_pairs={{0,1},{1,0},{2,3},{3,2},{4,5},{5,4},{6,7},{7,6},{8,9},{9,8},{10,11... | collective-permute-start | bytes 393224 | tf_op jit(solution)/shard_map/ppermute | solution.py:322
  32.3 3.9 %project_own.1.kept_ref = f32[4,8,2048]{2,1,0:T(8,128)S(1)} custom-call(bf16[8,1024]{1,0:T(8,128)(2,1)S(1)} %get-tuple-element.32.flat_ref, bf16[1,1024,16384]{2,1,0:T(8,128)(2,1)} %weight_ref.9, bf16[2,1024,1024]{2,1,0:T(8,128)(2,1)S(1)} %get-tuple-element.31.refs_5_.refs_0_, bf16[2,1024,1024]{2,1,0:T(8,128)(2,1)S(1)} %stage.3.after_ref.refs_6_.refs_1_, ...), custom_call_target="tpu_custom_call" | custom-call | flops 16777216 | bytes 16777216 | tf_op jit(solution)/shard_map/project_own/pallas_call | solution.py:291
  36.3 1.9 %collective-permute-start.9 = (bf16[2,8,2048]{2,1,0:T(8,128)(2,1)S(1)}, bf16[2,8,2048]{2,1,0:T(8,128)(2,1)S(1)}, u32[]{:S(2)}, u32[]{:S(2)}) collective-permute-start(bf16[2,8,2048]{2,1,0:T(8,128)(2,1)S(1)} %get-tuple-element.35), channel_id=1, source_target_pairs={{0,6},{1,7},{2,4},{3,5},{4,2},{5,3},{6,0},{7,1},{8,14},{9,15},{10,... | collective-permute-start | bytes 196616 | tf_op jit(solution)/shard_map/ppermute | solution.py:322
  38.3 2.5 %collective-permute-start.11 = (bf16[2,8,2048]{2,1,0:T(8,128)(2,1)S(1)}, bf16[2,8,2048]{2,1,0:T(8,128)(2,1)S(1)}, u32[]{:S(2)}, u32[]{:S(2)}) collective-permute-start(bf16[2,8,2048]{2,1,0:T(8,128)(2,1)S(1)} %get-tuple-element.37), channel_id=1, source_target_pairs={{0,2},{1,3},{2,0},{3,1},{4,6},{5,7},{6,4},{7,5},{8,10},{9,11},{10,... | collective-permute-start | bytes 196616 | tf_op jit(solution)/shard_map/ppermute | solution.py:322
  40.8 1.7 %collective-permute-done.9.three_ref = bf16[2,8,2048]{2,1,0:T(8,128)(2,1)S(1)} collective-permute-done((bf16[2,8,2048]{2,1,0:T(8,128)(2,1)S(1)}, bf16[2,8,2048]{2,1,0:T(8,128)(2,1)S(1)}, u32[]{:S(2)}, u32[]{:S(2)}) %collective-permute-start.9) | collective-permute-done | bytes 65568 | tf_op jit(solution)/shard_map/ppermute | solution.py:322
  42.5 1.4 %collective-permute-done.10.two_ref = bf16[2,8,2048]{2,1,0:T(8,128)(2,1)S(1)} collective-permute-done((bf16[2,8,2048]{2,1,0:T(8,128)(2,1)S(1)}, bf16[2,8,2048]{2,1,0:T(8,128)(2,1)S(1)}, u32[]{:S(2)}, u32[]{:S(2)}) %collective-permute-start.10) | collective-permute-done | bytes 65568 | tf_op jit(solution)/shard_map/ppermute | solution.py:322
  44.1 2.2 %collective-permute-start.14 = (bf16[2,8,2048]{2,1,0:T(8,128)(2,1)S(1)}, bf16[2,8,2048]{2,1,0:T(8,128)(2,1)S(1)}, u32[]{:S(2)}, u32[]{:S(2)}) collective-permute-start(bf16[2,8,2048]{2,1,0:T(8,128)(2,1)S(1)} %owner.1), channel_id=1, source_target_pairs={{0,10},{1,11},{2,8},{3,9},{4,14},{5,15},{6,12},{7,13},{8,2},{9,3},... | collective-permute-start | bytes 196616 | tf_op jit(solution)/shard_map/ppermute | solution.py:322
  46.5 1.0 %collective-permute-start.12 = (bf16[2,8,2048]{2,1,0:T(8,128)(2,1)S(1)}, bf16[2,8,2048]{2,1,0:T(8,128)(2,1)S(1)}, u32[]{:S(2)}, u32[]{:S(2)}) collective-permute-start(bf16[2,8,2048]{2,1,0:T(8,128)(2,1)S(1)} %owner.1), channel_id=1, source_target_pairs={{0,8},{1,9},{2,10},{3,11},{4,12},{5,13},{6,14},{7,15},{8,0},{9,1},... | collective-permute-start | bytes 196616 | tf_op jit(solution)/shard_map/ppermute | solution.py:322
  47.4 1.3 %collective-permute-done.15.refs_3_ = bf16[2,8,2048]{2,1,0:T(8,128)(2,1)S(1)} collective-permute-done((bf16[2,8,2048]{2,1,0:T(8,128)(2,1)S(1)}, bf16[2,8,2048]{2,1,0:T(8,128)(2,1)S(1)}, u32[]{:S(2)}, u32[]{:S(2)}) %collective-permute-start.15) | collective-permute-done | bytes 65568 | tf_op jit(solution)/shard_map/ppermute | solution.py:322
  48.9 1.5 %collective-permute-done.13.refs_1_ = bf16[2,8,2048]{2,1,0:T(8,128)(2,1)S(1)} collective-permute-done((bf16[2,8,2048]{2,1,0:T(8,128)(2,1)S(1)}, bf16[2,8,2048]{2,1,0:T(8,128)(2,1)S(1)}, u32[]{:S(2)}, u32[]{:S(2)}) %collective-permute-start.13) | collective-permute-done | bytes 65568 | tf_op jit(solution)/shard_map/ppermute | solution.py:322
  50.4 0.7 %placed.1 = bf16[1,8,16384]{2,1,0:T(8,128)(2,1)} custom-call(bf16[2,8,2048]{2,1,0:T(8,128)(2,1)S(1)} %collective-permute-done.12.refs_0_, bf16[2,8,2048]{2,1,0:T(8,128)(2,1)S(1)} %collective-permute-done.13.refs_1_, bf16[2,8,2048]{2,1,0:T(8,128)(2,1)S(1)} %collective-permute-done.14.refs_2_, bf16[2,8,2048]{2,1,0:T(8,128)(2,1)S(1)} %collective-permute-done.15.refs_3_), custom_call_target="tpu_custom_call" | custom-call | flops 1048576 | bytes 1048576 | tf_op jit(solution)/shard_map/placed/pallas_call | solution.py:291
  (22 shorter events, 1.1 us)
Async XLA Ops:
  0.0 5.9 %collective-permute-start = (bf16[1,8,8,128]{3,2,1,0:T(8,128)(2,1)}, bf16[1,8,8,128]{3,2,1,0:T(8,128)(2,1)S(1)}, u32[]{:S(2)}, u32[]{:S(2)}) collective-permute-start(bf16[1,8,8,128]{3,2,1,0:T(8,128)(2,1)} %queries_ref.1), channel_id=1, source_target_pairs={{0,1},{1,0},{2,3},{3,2},{4,5},{5,4},{6,7},{7,6},{8,9},{9,8},{10,11... | collective-permute-start | bytes 49160 | tf_op jit(solution)/shard_map/ppermute | solution.py:322
  5.9 6.7 %collective-permute-start.3 = (bf16[2,8,8,128]{3,2,1,0:T(8,128)(2,1)S(1)}, bf16[2,8,8,128]{3,2,1,0:T(8,128)(2,1)S(1)}, u32[]{:S(2)}, u32[]{:S(2)}) collective-permute-start(bf16[2,8,8,128]{3,2,1,0:T(8,128)(2,1)S(1)} %append.1.after_ref.refs_0_), channel_id=1, source_target_pairs={{0,6},{1,7},{2,4},{3,5},{4,2},{5,3},{6,0},{7,1},{8,14},{9,15},{10,... | collective-permute-start | bytes 98312 | tf_op jit(solution)/shard_map/ppermute | solution.py:322
  9.6 4.8 %collective-permute-start.2 = (bf16[2,8,8,128]{3,2,1,0:T(8,128)(2,1)S(1)}, bf16[2,8,8,128]{3,2,1,0:T(8,128)(2,1)S(1)}, u32[]{:S(2)}, u32[]{:S(2)}) collective-permute-start(bf16[2,8,8,128]{3,2,1,0:T(8,128)(2,1)S(1)} %append.1.after_ref.refs_0_), channel_id=1, source_target_pairs={{0,4},{1,5},{2,6},{3,7},{4,0},{5,1},{6,2},{7,3},{8,12},{9,13},{10,... | collective-permute-start | bytes 98312 | tf_op jit(solution)/shard_map/ppermute | solution.py:322
  9.6 4.8 %collective-permute-start.1 = (bf16[2,8,8,128]{3,2,1,0:T(8,128)(2,1)S(1)}, bf16[2,8,8,128]{3,2,1,0:T(8,128)(2,1)S(1)}, u32[]{:S(2)}, u32[]{:S(2)}) collective-permute-start(bf16[2,8,8,128]{3,2,1,0:T(8,128)(2,1)S(1)} %append.1.after_ref.refs_0_), channel_id=1, source_target_pairs={{0,2},{1,3},{2,0},{3,1},{4,6},{5,7},{6,4},{7,5},{8,10},{9,11},{10,... | collective-permute-start | bytes 98312 | tf_op jit(solution)/shard_map/ppermute | solution.py:322
  15.5 4.5 %collective-permute-start.4 = (bf16[4,80,128]{2,1,0:T(8,128)(2,1)S(1)}, bf16[4,80,128]{2,1,0:T(8,128)(2,1)S(1)}, u32[]{:S(2)}, u32[]{:S(2)}) collective-permute-start(bf16[4,80,128]{2,1,0:T(8,128)(2,1)S(1)} %get-tuple-element.25.after_ref), channel_id=1, source_target_pairs={{0,1},{1,0},{2,3},{3,2},{4,5},{5,4},{6,7},{7,6},{8,9},{9,8},{10,11... | collective-permute-start | bytes 245768 | tf_op jit(solution)/shard_map/ppermute | solution.py:322
  20.2 8.0 %collective-permute-start.5 = (bf16[1,80,128]{2,1,0:T(8,128)(2,1)S(1)}, bf16[1,80,128]{2,1,0:T(8,128)(2,1)S(1)}, u32[]{:S(2)}, u32[]{:S(2)}) collective-permute-start(bf16[1,80,128]{2,1,0:T(8,128)(2,1)S(1)} %get-tuple-element.28), channel_id=1, source_target_pairs={{0,6},{1,7},{2,4},{3,5},{4,2},{5,3},{6,0},{7,1},{8,14},{9,15},{10,... | collective-permute-start | bytes 61448 | tf_op jit(solution)/shard_map/ppermute | solution.py:322
  22.2 6.1 %collective-permute-start.6 = (bf16[1,80,128]{2,1,0:T(8,128)(2,1)S(1)}, bf16[1,80,128]{2,1,0:T(8,128)(2,1)S(1)}, u32[]{:S(2)}, u32[]{:S(2)}) collective-permute-start(bf16[1,80,128]{2,1,0:T(8,128)(2,1)S(1)} %get-tuple-element.29), channel_id=1, source_target_pairs={{0,4},{1,5},{2,6},{3,7},{4,0},{5,1},{6,2},{7,3},{8,12},{9,13},{10,... | collective-permute-start | bytes 61448 | tf_op jit(solution)/shard_map/ppermute | solution.py:322
  22.4 5.8 %collective-permute-start.7 = (bf16[1,80,128]{2,1,0:T(8,128)(2,1)S(1)}, bf16[1,80,128]{2,1,0:T(8,128)(2,1)S(1)}, u32[]{:S(2)}, u32[]{:S(2)}) collective-permute-start(bf16[1,80,128]{2,1,0:T(8,128)(2,1)S(1)} %get-tuple-element.30.after_ref), channel_id=1, source_target_pairs={{0,2},{1,3},{2,0},{3,1},{4,6},{5,7},{6,4},{7,5},{8,10},{9,11},{10,... | collective-permute-start | bytes 61448 | tf_op jit(solution)/shard_map/ppermute | solution.py:322
  31.2 5.1 %collective-permute-start.8 = (bf16[4,8,2048]{2,1,0:T(8,128)(2,1)S(1)}, bf16[4,8,2048]{2,1,0:T(8,128)(2,1)S(1)}, u32[]{:S(2)}, u32[]{:S(2)}) collective-permute-start(bf16[4,8,2048]{2,1,0:T(8,128)(2,1)S(1)} %get-tuple-element.34), channel_id=1, source_target_pairs={{0,1},{1,0},{2,3},{3,2},{4,5},{5,4},{6,7},{7,6},{8,9},{9,8},{10,11... | collective-permute-start | bytes 393224 | tf_op jit(solution)/shard_map/ppermute | solution.py:322
  32.3 4.0 %copy-start = (bf16[1,8,2048]{2,1,0:T(8,128)(2,1)S(1)}, bf16[1,8,2048]{2,1,0:T(8,128)(2,1)}, u32[]{:S(2)}) copy-start(bf16[1,8,2048]{2,1,0:T(8,128)(2,1)} %residual_ref.1) | copy-start | bytes 98308
  36.3 6.1 %collective-permute-start.9 = (bf16[2,8,2048]{2,1,0:T(8,128)(2,1)S(1)}, bf16[2,8,2048]{2,1,0:T(8,128)(2,1)S(1)}, u32[]{:S(2)}, u32[]{:S(2)}) collective-permute-start(bf16[2,8,2048]{2,1,0:T(8,128)(2,1)S(1)} %get-tuple-element.35), channel_id=1, source_target_pairs={{0,6},{1,7},{2,4},{3,5},{4,2},{5,3},{6,0},{7,1},{8,14},{9,15},{10,... | collective-permute-start | bytes 196616 | tf_op jit(solution)/shard_map/ppermute | solution.py:322
  38.3 5.6 %collective-permute-start.10 = (bf16[2,8,2048]{2,1,0:T(8,128)(2,1)S(1)}, bf16[2,8,2048]{2,1,0:T(8,128)(2,1)S(1)}, u32[]{:S(2)}, u32[]{:S(2)}) collective-permute-start(bf16[2,8,2048]{2,1,0:T(8,128)(2,1)S(1)} %get-tuple-element.36), channel_id=1, source_target_pairs={{0,4},{1,5},{2,6},{3,7},{4,0},{5,1},{6,2},{7,3},{8,12},{9,13},{10,... | collective-permute-start | bytes 196616 | tf_op jit(solution)/shard_map/ppermute | solution.py:322
  38.3 5.6 %collective-permute-start.11 = (bf16[2,8,2048]{2,1,0:T(8,128)(2,1)S(1)}, bf16[2,8,2048]{2,1,0:T(8,128)(2,1)S(1)}, u32[]{:S(2)}, u32[]{:S(2)}) collective-permute-start(bf16[2,8,2048]{2,1,0:T(8,128)(2,1)S(1)} %get-tuple-element.37), channel_id=1, source_target_pairs={{0,2},{1,3},{2,0},{3,1},{4,6},{5,7},{6,4},{7,5},{8,10},{9,11},{10,... | collective-permute-start | bytes 196616 | tf_op jit(solution)/shard_map/ppermute | solution.py:322
  44.0 4.7 %collective-permute-start.15 = (bf16[2,8,2048]{2,1,0:T(8,128)(2,1)S(1)}, bf16[2,8,2048]{2,1,0:T(8,128)(2,1)S(1)}, u32[]{:S(2)}, u32[]{:S(2)}) collective-permute-start(bf16[2,8,2048]{2,1,0:T(8,128)(2,1)S(1)} %owner.1), channel_id=1, source_target_pairs={{0,11},{1,10},{2,9},{3,8},{4,15},{5,14},{6,13},{7,12},{8,3},{9,2},... | collective-permute-start | bytes 196616 | tf_op jit(solution)/shard_map/ppermute | solution.py:322
  44.1 4.8 %collective-permute-start.14 = (bf16[2,8,2048]{2,1,0:T(8,128)(2,1)S(1)}, bf16[2,8,2048]{2,1,0:T(8,128)(2,1)S(1)}, u32[]{:S(2)}, u32[]{:S(2)}) collective-permute-start(bf16[2,8,2048]{2,1,0:T(8,128)(2,1)S(1)} %owner.1), channel_id=1, source_target_pairs={{0,10},{1,11},{2,8},{3,9},{4,14},{5,15},{6,12},{7,13},{8,2},{9,3},... | collective-permute-start | bytes 196616 | tf_op jit(solution)/shard_map/ppermute | solution.py:322
  46.3 4.1 %collective-permute-start.13 = (bf16[2,8,2048]{2,1,0:T(8,128)(2,1)S(1)}, bf16[2,8,2048]{2,1,0:T(8,128)(2,1)S(1)}, u32[]{:S(2)}, u32[]{:S(2)}) collective-permute-start(bf16[2,8,2048]{2,1,0:T(8,128)(2,1)S(1)} %owner.1), channel_id=1, source_target_pairs={{0,9},{1,8},{2,11},{3,10},{4,13},{5,12},{6,15},{7,14},{8,1},{9,0},... | collective-permute-start | bytes 196616 | tf_op jit(solution)/shard_map/ppermute | solution.py:322
  46.5 3.9 %collective-permute-start.12 = (bf16[2,8,2048]{2,1,0:T(8,128)(2,1)S(1)}, bf16[2,8,2048]{2,1,0:T(8,128)(2,1)S(1)}, u32[]{:S(2)}, u32[]{:S(2)}) collective-permute-start(bf16[2,8,2048]{2,1,0:T(8,128)(2,1)S(1)} %owner.1), channel_id=1, source_target_pairs={{0,8},{1,9},{2,10},{3,11},{4,12},{5,13},{6,14},{7,15},{8,0},{9,1},... | collective-permute-start | bytes 196616 | tf_op jit(solution)/shard_map/ppermute | solution.py:322
